TPU v7x, 32 devices: a whole 2x2x4 slice. The times are simulated.
32 devices in a mesh: shot: 16 (over z, y, core), tm: 2 (over x).
Axes of the slice: x: 2, y: 2, z: 4, core: 2. Of those that a mesh axis runs over, the one named last changes fastest.
Arguments:
- blended: float32 [64, 32, 2048], P(None, 'shot', 'tm'), may hold values from -12 to 12
- delays: int32 [32, 2], replicated, may hold values from 0 to 127, as said below
- thresholds: float32 [2, 64], replicated, may hold values from 0.2 to 1.6
Outputs:
- deblended: bfloat16 [64, 64, 2048], P(None, 'shot', 'tm')
Inputs may be any that keep to these rules, and one draw needn't show every extreme that they name: delays[e, k] is the delay of source 2 e + k in experiment e; some source has delay 0 and some has delay 128 - 1.
All inputs are finite; a program needn't handle non-finite values.
Results may differ from a plain program's by a relative error of at most 0.0066.
Values may be sent and summed in bfloat16 or wider, within the bound.
No kernel may reach another device: no remote copies, remote signals or barrier semaphores. Data moves between devices by JAX's collectives and lax.ppermute only.
A program may use at most 64 MiB of HBM per device.

v0:
```python
import functools
import math

import jax
import jax.numpy as jnp
import ml_dtypes
import numpy as np
from jax import lax
from jax.experimental import pallas as pl
from jax.experimental.pallas import tpu as pltpu
from jax.sharding import PartitionSpec as P

SRC = 64
SRC_EXP = 2
WIN = 256
BLK = 128
ITERS = 2


RELAX = 0.5
HALF = WIN // 2
SUB = 8


def split_table(table):
    high = table.astype(ml_dtypes.bfloat16)
    low = (table - high.astype(np.float64)).astype(ml_dtypes.bfloat16)
    return high, low


def half_spectrum_tables():
    moment = np.arange(WIN)
    angle = (moment[:, None] * np.arange(HALF)[None, :] % WIN) * (2.0 * math.pi / WIN)
    nyquist = np.where(moment % 2 == 0, 1.0, -1.0)
    sine = -np.sin(angle)
    sine[:, 0] = nyquist
    forward = np.concatenate([np.cos(angle), sine], axis=1).astype(ml_dtypes.bfloat16)
    inverse = np.concatenate([np.cos(angle), sine], axis=1).T / math.sqrt(WIN)
    inverse[0] *= 0.5
    inverse[HALF] *= 0.5
    source = np.arange(SRC)
    turn = (source[:, None] * source[None, :] % SRC) * (2.0 * math.pi / SRC)
    cosine, sine = np.cos(turn) / math.sqrt(SRC), np.sin(turn) / math.sqrt(SRC)
    onward = np.block([[cosine, sine], [-sine, cosine]])
    pair = []
    for table in (onward / math.sqrt(WIN), onward.T):
        high, low = split_table(table)
        pair.append(np.block([[high, high], [low, low]]))
    return (forward, *split_table(inverse), *pair)


def halves(value):
    high = value.astype(jnp.bfloat16)
    return high, (value - high.astype(jnp.float32)).astype(jnp.bfloat16)


def bfloat(value):
    return value.astype(jnp.bfloat16).astype(jnp.float32)


def product(left, right):
    return jnp.dot(left, right, preferred_element_type=jnp.float32)


def gather_kernel(
    shots,
    delays,
    limits,
    received,
    forward,
    inverse_high,
    inverse_low,
    onward,
    backward,
    out,
    records,
    field,
    mixed,
    back_high,
    back_low,
    traces,
):
    count, receivers, rows, _ = received.shape
    blocks_of_time = count // shots
    experiments, sources = delays.shape[0], SRC
    own = experiments // shots
    windows = records.shape[2] // (2 * own)
    groups = receivers * windows
    parts = windows // blocks_of_time
    lane = lax.broadcasted_iota(jnp.int32, (windows, BLK), 1)
    row = lax.broadcasted_iota(jnp.int32, (windows, BLK), 0)
    lane_of_group = lax.broadcasted_iota(jnp.int32, (sources, HALF), 1)

    for shot in range(shots):
        for block in range(blocks_of_time):
            arrived = received[shot * blocks_of_time + block].astype(jnp.float32)
            for r in range(receivers):
                records[r, shot, block * rows : (block + 1) * rows, :] = arrived[r]

    def record(r, shot, e):
        return tuple(
            records[r, shot, pl.ds(half * own + e, windows, stride=2 * own), :]
            for half in range(2)
        )

    def trace_rows(r, s):
        return pl.ds(r * windows * sources + s, windows, stride=sources)

    def load(r, s):
        return tuple(traces[half, trace_rows(r, s), :] for half in range(2))

    def store(r, s, values):
        for half in range(2):
            traces[half, trace_rows(r, s), :] = values[half]

    def advanced(even, odd, delay):
        by = (BLK - delay) & (BLK - 1)
        even, odd = pltpu.roll(even, by, 1), pltpu.roll(odd, by, 1)
        after = jnp.where(row < windows - 1, pltpu.roll(even, windows - 1, 0), 0.0)
        same = lane < BLK - delay
        return jnp.where(same, even, odd), jnp.where(same, odd, after)

    def delayed(even, odd, delay):
        even, odd = pltpu.roll(even, delay, 1), pltpu.roll(odd, delay, 1)
        before = jnp.where(row > 0, pltpu.roll(odd, 1, 0), 0.0)
        same = lane >= delay
        return jnp.where(same, even, before), jnp.where(same, odd, even)

    def update(sweep):
        def one(shot, carry):
            for e in range(own):
                first = (shot * own + e) * SRC_EXP
                lags = [delays[shot * own + e, k] for k in range(SRC_EXP)]
                for r in range(receivers):
                    even, odd = record(r, shot, e)
                    if sweep > 0:
                        estimate = [load(r, first + k) for k in range(SRC_EXP)]
                        late = [delayed(*estimate[k], lags[k]) for k in range(SRC_EXP)]
                        even = bfloat(even - sum(x[0] for x in late))
                        odd = bfloat(odd - sum(x[1] for x in late))
                    for k in range(SRC_EXP):
                        early = advanced(even, odd, lags[k])
                        values = [RELAX * x for x in early]
                        if sweep > 0:
                            values = [a + b for a, b in zip(estimate[k], values)]
                        store(r, first + k, values)
            return carry

        lax.fori_loop(0, shots, one, 0, unroll=2)

    def columns(group, many=1):
        return slice(group * HALF, (group + many) * HALF)

    def forward_in_time():
        nyquist = jnp.zeros((sources, HALF), jnp.float32)
        for group in range(groups):
            rows_of_group = slice(group * sources, (group + 1) * sources)
            signal = jnp.concatenate([traces[half, rows_of_group, :] for half in range(2)], axis=1)
            signal = signal.astype(jnp.bfloat16)
            spectrum = product(signal, forward[...])
            real, imag = spectrum[:, :HALF], spectrum[:, HALF:]
            moved = pltpu.roll(imag, group, 1) if group else imag
            nyquist = jnp.where(lane_of_group == group, moved, nyquist)
            imag = jnp.where(lane_of_group == 0, 0.0, imag)
            put(field, columns(group), real, imag)
        put(field, columns(groups), nyquist, jnp.zeros_like(nyquist))

    def put(ref, where, real, imag):
        real_high, real_low = halves(real)
        imag_high, imag_low = halves(imag)
        for at, value in enumerate((real_high, imag_high, real_low, imag_low)):
            ref[at * sources : (at + 1) * sources, where] = value

    def chunks():
        yield columns(groups)
        for group in range(0, groups, 2):
            yield columns(group, 2)

    def mixing(table, ref, where):
        both = product(table[...], ref[:, where])
        total = both[: 2 * sources] + both[2 * sources :]
        return total[:sources], total[sources:]

    def shrink(sweep):
        limit = limits[sweep : sweep + 1, :]
        p = lax.broadcasted_iota(jnp.int32, (sources, sources), 0)
        q = lax.broadcasted_iota(jnp.int32, (sources, sources), 1)
        bound = jnp.sum(jnp.where(p == q, limit, 0.0), axis=1, keepdims=True)
        mirrored = (p + q == 0) | (p + q == sources)
        bound_mirrored = jnp.sum(jnp.where(mirrored, limit, 0.0), axis=1, keepdims=True)
        for where in chunks():
            real, imag = mixing(onward, field, where)
            inverse_size = lax.rsqrt(real * real + imag * imag)
            factor = jnp.maximum(1.0 - bound * inverse_size, 0.0) + jnp.maximum(
                1.0 - bound_mirrored * inverse_size, 0.0
            )
            put(mixed, where, real * factor, imag * factor)

    def back_in_source():
        nyquist = None
        group = 0
        for where in chunks():
            real, imag = mixing(backward, mixed, where)
            if nyquist is None:
                nyquist = real
                continue
            for part in range(2):
                own_real, own_imag = real[:, columns(part)], imag[:, columns(part)]
                moved = pltpu.roll(nyquist, HALF - group, 1) if group else nyquist
                own_imag = jnp.where(lane_of_group == 0, moved, own_imag)
                rows_of_group = slice(group * sources, (group + 1) * sources)
                for half, value in enumerate((own_real, own_imag)):
                    high, low = halves(value)
                    back_high[rows_of_group, columns(half)] = high
                    back_low[rows_of_group, columns(half)] = low
                group += 1

    def back_in_time(rows_of_pair):
        high = back_high[rows_of_pair, :]
        return (
            product(high, inverse_high[...])
            + product(back_low[rows_of_pair, :], inverse_high[...])
            + product(high, inverse_low[...])
        )

    def swapped(value):
        return pltpu.roll(value, SUB // 2, 1)

    def deliver(r, w, restored):
        low = lax.broadcasted_iota(jnp.int32, (sources // SUB, SUB, BLK), 1) < SUB // 2
        pieces = []
        for part in range(2):
            window = restored[part * sources : (part + 1) * sources]
            even = window[:, :BLK].reshape(sources // SUB, SUB, BLK)
            odd = window[:, BLK:].reshape(sources // SUB, SUB, BLK)
            pieces.append(
                (jnp.where(low, even, swapped(odd)), jnp.where(low, swapped(even), odd))
            )
        block, inside = w // parts, w % parts
        for side in range(2):
            both = jnp.concatenate([pieces[0][side], pieces[1][side]], axis=1)
            both = both.astype(jnp.bfloat16)
            for k in range(sources // SUB):
                target = (2 * k + side) * blocks_of_time + block
                out[target, r, inside * SUB : (inside + 2) * SUB, :] = both[k]

    for sweep in range(ITERS):
        update(sweep)
        forward_in_time()
        shrink(sweep)
        back_in_source()
        for group in range(0, groups, 2):
            rows_of_pair = slice(group * sources, (group + 2) * sources)
            restored = back_in_time(rows_of_pair)
            if sweep < ITERS - 1:
                for half in range(2):
                    traces[half, rows_of_pair, :] = bfloat(restored[:, columns(half)])
            else:
                deliver(group // windows, group % windows, restored)


def gathers_of_all_samples(shots, blended, delays, thresholds):
    receivers, own, samples = blended.shape
    blocks_of_time = lax.axis_size("tm")
    count = shots * blocks_of_time
    each = receivers // count
    blocks = samples // BLK
    windows = samples * blocks_of_time // WIN
    groups = each * windows
    rows = blocks * own
    sent = blended.reshape(receivers, own, blocks, BLK).transpose(0, 2, 1, 3)
    sent = sent.astype(jnp.bfloat16).reshape(count, each, rows, BLK)
    received = lax.all_to_all(sent, ("shot", "tm"), split_axis=0, concat_axis=0, tiled=True)
    tables = [jnp.asarray(table) for table in half_spectrum_tables()]
    vmem = pl.BlockSpec(memory_space=pltpu.VMEM)
    held = SRC // shots
    restored = pl.pallas_call(
        functools.partial(gather_kernel, shots),
        out_shape=jax.ShapeDtypeStruct((count, each, blocks * held, BLK), jnp.bfloat16),
        in_specs=[pl.BlockSpec(memory_space=pltpu.SMEM)] + [vmem] * 7,
        out_specs=vmem,
        scratch_shapes=[
            pltpu.VMEM((each, shots, blocks_of_time * rows, BLK), jnp.float32),
            pltpu.VMEM((4 * SRC, (groups + 1) * HALF), jnp.bfloat16),
            pltpu.VMEM((4 * SRC, (groups + 1) * HALF), jnp.bfloat16),
            pltpu.VMEM((groups * SRC, WIN), jnp.bfloat16),
            pltpu.VMEM((groups * SRC, WIN), jnp.bfloat16),
            pltpu.VMEM((2, groups * SRC, BLK), jnp.float32),
        ],
        compiler_params=pltpu.CompilerParams(vmem_limit_bytes=40 * 1024 * 1024),
        cost_estimate=pl.CostEstimate(
            flops=2 * ITERS * groups * SRC * WIN * WIN * 9,
            bytes_accessed=2 * 1024 * 1024,
            transcendentals=ITERS * groups * SRC * HALF,
        ),
    )(delays, thresholds, received, *tables)
    final = lax.all_to_all(restored, ("shot", "tm"), split_axis=0, concat_axis=0, tiled=True)
    final = final.reshape(receivers, blocks, held, BLK).transpose(0, 2, 1, 3)
    return final.reshape(receivers, held, samples)


def shifted(array, axis, by):
    count = lax.axis_size(axis)
    pairs = [(i, i + by) for i in range(count) if 0 <= i + by < count]
    return lax.ppermute(array, axis, pairs)


def phase_table(length_first, length_second, period):
    first_index = jnp.arange(length_first, dtype=jnp.int32)[:, None]
    second_index = jnp.arange(length_second, dtype=jnp.int32)[None, :]
    return (first_index * second_index % period).astype(jnp.float32) * (2.0 * math.pi / period)


def make_tables():
    time_angle = phase_table(WIN, WIN, WIN)
    time_scale = 1.0 / math.sqrt(WIN)
    cos_forward = jnp.cos(time_angle).astype(jnp.bfloat16)
    sin_forward = -jnp.sin(time_angle).astype(jnp.bfloat16)
    cos_inverse = jnp.cos(time_angle) * time_scale
    sin_inverse = -jnp.sin(time_angle) * time_scale
    source_angle = phase_table(SRC, SRC, SRC)
    cos_source = jnp.cos(source_angle) / math.sqrt(SRC)
    sin_source = jnp.sin(source_angle) / math.sqrt(SRC)
    return (cos_forward, sin_forward, cos_inverse, sin_inverse, cos_source, sin_source)


def blend(estimate, own_delays):
    receivers, sources, samples = estimate.shape
    blocks = samples // BLK
    experiments = sources // SRC_EXP
    earlier = shifted(estimate[:, :, samples - BLK :], "tm", 1)
    upper = estimate.reshape(receivers, sources, blocks, BLK)
    shifts = own_delays.reshape(-1)
    row_index = jnp.arange(BLK, dtype=jnp.int32)[None, :, None]
    column_index = jnp.arange(BLK, dtype=jnp.int32)[None, None, :]
    select_same = (row_index == column_index - shifts[:, None, None]).astype(jnp.bfloat16)
    select_prior = (row_index == BLK + column_index - shifts[:, None, None]).astype(jnp.bfloat16)
    same = jnp.einsum("rsnb,sbi->rsni", upper, select_same, preferred_element_type=jnp.float32)
    onward = jnp.einsum("rsnb,sbi->rsni", upper, select_prior, preferred_element_type=jnp.float32)
    edge_part = jnp.einsum(
        "rsb,sbi->rsi", earlier, select_prior, preferred_element_type=jnp.float32
    )
    same = jnp.sum(same.reshape(receivers, experiments, SRC_EXP, blocks, BLK), axis=2)
    onward = jnp.sum(onward.reshape(receivers, experiments, SRC_EXP, blocks, BLK), axis=2)
    edge_part = jnp.sum(edge_part.reshape(receivers, experiments, SRC_EXP, BLK), axis=2)
    carried = jnp.concatenate([edge_part[:, :, None], onward[:, :, : blocks - 1]], axis=2)
    return (same + carried).reshape(receivers, experiments, samples)


def spread(residual, own_delays):
    receivers, experiments, samples = residual.shape
    blocks = samples // BLK
    later = shifted(residual[:, :, :BLK], "tm", -1)
    lower = residual.reshape(receivers, experiments, blocks, BLK)
    row_index = jnp.arange(BLK, dtype=jnp.int32)[None, None, :, None]
    column_index = jnp.arange(BLK, dtype=jnp.int32)[None, None, None, :]
    select_same = (row_index == column_index + own_delays[:, :, None, None]).astype(jnp.bfloat16)
    select_next = (row_index + BLK == column_index + own_delays[:, :, None, None]).astype(
        jnp.bfloat16
    )
    same = jnp.einsum("rena,ekai->rekni", lower, select_same, preferred_element_type=jnp.float32)
    backward = jnp.einsum(
        "rena,ekai->rekni", lower, select_next, preferred_element_type=jnp.float32
    )
    edge_part = jnp.einsum("rea,ekai->reki", later, select_next, preferred_element_type=jnp.float32)
    carried = jnp.concatenate([backward[:, :, :, 1:], edge_part[:, :, :, None]], axis=3)
    return (same + carried).reshape(receivers, experiments * SRC_EXP, samples)


def coherence(gathers, limits, tables):
    cos_forward, sin_forward, cos_inverse, sin_inverse, cos_source, sin_source = tables
    receivers, sources, samples = gathers.shape
    windows = samples // WIN
    careful = lax.Precision.HIGH
    scale = 1.0 / math.sqrt(WIN)
    signal = gathers.reshape(receivers * sources * windows, WIN)
    real_time = (jnp.dot(signal, cos_forward, preferred_element_type=jnp.float32) * scale).reshape(
        receivers, sources, samples
    )
    imag_time = (jnp.dot(signal, sin_forward, preferred_element_type=jnp.float32) * scale).reshape(
        receivers, sources, samples
    )

    def mixing(table, field):
        return jnp.einsum(
            "ps,rsx->rpx", table, field, precision=careful, preferred_element_type=jnp.float32
        )

    real_part = mixing(cos_source, real_time) + mixing(sin_source, imag_time)
    imag_part = mixing(cos_source, imag_time) - mixing(sin_source, real_time)
    magnitude = jnp.sqrt(real_part * real_part + imag_part * imag_part)
    bound = limits[None, :, None]
    factor = jnp.maximum(magnitude - bound, 0.0) / jnp.maximum(magnitude, bound)
    kept_real = real_part * factor
    kept_imag = imag_part * factor
    back_real = mixing(cos_source, kept_real) - mixing(sin_source, kept_imag)
    back_imag = mixing(cos_source, kept_imag) + mixing(sin_source, kept_real)
    restored = jnp.dot(
        back_real.reshape(-1, WIN),
        cos_inverse,
        precision=careful,
        preferred_element_type=jnp.float32,
    )
    restored = restored + jnp.dot(
        back_imag.reshape(-1, WIN),
        sin_inverse,
        precision=careful,
        preferred_element_type=jnp.float32,
    )
    return restored.reshape(receivers, sources, samples)


def gathers_of_own_samples(blended, delays, thresholds):
    tables = make_tables()
    local_count = blended.shape[1]
    own_delays = lax.dynamic_slice_in_dim(
        delays, lax.axis_index("shot") * local_count, local_count, 0
    )
    estimate = None
    for sweep in range(ITERS):
        if sweep == 0:
            residual = blended.astype(jnp.bfloat16)
            update = (RELAX * spread(residual, own_delays)).astype(jnp.bfloat16)
        else:
            residual = (blended - blend(estimate, own_delays)).astype(jnp.bfloat16)
            update = (estimate.astype(jnp.float32) + RELAX * spread(residual, own_delays)).astype(
                jnp.bfloat16
            )
        gathers = lax.all_to_all(update, "shot", split_axis=0, concat_axis=1, tiled=True)
        filtered = coherence(gathers, thresholds[sweep], tables).astype(jnp.bfloat16)
        estimate = lax.all_to_all(filtered, "shot", split_axis=1, concat_axis=0, tiled=True)
    return estimate


def whole_receivers_fit(shots, blocks_of_time, receivers, samples):
    held, windows = SRC // shots, samples // WIN
    return (
        receivers % (shots * blocks_of_time) == 0
        and held * 2 == SUB
        and windows % 2 == 0
        and windows * blocks_of_time == SUB
        and receivers // (shots * blocks_of_time) * SUB <= HALF
    )


def local(blended, delays, thresholds):
    shots, blocks_of_time = lax.axis_size("shot"), lax.axis_size("tm")
    if whole_receivers_fit(shots, blocks_of_time, blended.shape[0], blended.shape[2]):
        return gathers_of_all_samples(shots, blended, delays, thresholds)
    return gathers_of_own_samples(blended, delays, thresholds)


def solution(mesh):
    return jax.shard_map(
        local,
        mesh=mesh,
        in_specs=(P(None, "shot", "tm"), P(), P()),
        out_specs=P(None, "shot", "tm"),
        check_vma=False,
    )
```

profile of v0, /device:TPU:1, one launch (start us, length us, event | category | flops | bytes accessed | tf_op | source)
XLA Modules:
  0.0 47.4 jit_solution(724377403153827125)
XLA Ops:
  0.0 0.0 copy-start.6
  0.0 0.0 copy-start.5
  0.0 2.0 %convert_element_type.9 = bf16[64,2,1024]{2,1,0:T(2,128)(2,1)} convert(f32[64,2,1024]{2,1,0:T(2,128)} %param.8) | non-fusion elementwise | flops 131072 | bytes 786432 | tf_op jit(solution)/shard_map/convert_element_type | solution.py:272
  2.0 0.0 copy-start.1
  2.0 0.0 copy-start.2
  2.0 0.0 copy-start.3
  2.0 0.0 copy-start.4
  2.0 7.1 %all-to-all-start = ((bf16[32,2,16,128]{3,2,1,0:T(8,128)(2,1)}), bf16[32,2,16,128]{3,2,1,0:T(8,128)(2,1)S(1)}, u32[]{:S(2)}, u32[]{:S(2)}) async-start(bf16[32,2,16,128]{3,2,1,0:T(8,128)(2,1)} %bitcast.2), calls=%async_computation | async-start | bytes 524288 | tf_op jit(solution)/shard_map/all_to_all | solution.py:273
  9.1 0.0 copy-done.6
  9.1 0.0 copy-start
  9.1 0.1 copy.10.delays
  9.2 10.4 %all-to-all-done.received = bf16[32,2,16,128]{3,2,1,0:T(8,128)(2,1)S(1)} async-done(((bf16[32,2,16,128]{3,2,1,0:T(8,128)(2,1)}), bf16[32,2,16,128]{3,2,1,0:T(8,128)(2,1)S(1)}, u32[]{:S(2)}, u32[]{:S(2)}) %all-to-all-start) | async-done | bytes 262176 | tf_op jit(solution)/shard_map/all_to_all | solution.py:273
  19.6 0.0 copy-done.5
  19.6 0.0 copy-done.1
  19.6 0.0 copy-done.2
  19.6 0.0 copy-done.3
  19.7 0.0 copy-done.4
  19.7 0.0 copy-done
  19.7 8.8 %shard_map.82 = bf16[32,2,32,128]{3,2,1,0:T(8,128)(2,1)S(1)} custom-call(s32[32,2]{1,0:T(8,128)S(1)} %copy.10.delays, f32[2,64]{1,0:T(2,128)S(1)} %copy-done, bf16[32,2,16,128]{3,2,1,0:T(8,128)(2,1)S(1)} %all-to-all-done.received, bf16[256,256]{1,0:T(8,128)(2,1)S(1)} %copy-done.5, bf16[256,256]{1,0:T(8,128)(2,1)S(1)} %copy-done.4, ...), custom_call_target="tpu_custom_call" | custom-call | flops 2415919104 | bytes 2097152 | tf_op jit(solution)/shard_map/pallas_call | solution.py:277
  28.5 18.1 %all_to_all.10 = bf16[32,2,32,128]{3,2,1,0:T(8,128)(2,1)S(1)} all-to-all(bf16[32,2,32,128]{3,2,1,0:T(8,128)(2,1)S(1)} %shard_map.82), channel_id=1, replica_groups=mesh['shot'=16,'tm'=2] {'shot','tm'}, dimensions={0} | all-to-all | bytes 1048576 | tf_op jit(solution)/shard_map/all_to_all | solution.py:297
  46.6 0.8 %copy.13 = bf16[64,4,1024]{2,1,0:T(4,128)(2,1)} copy(bf16[64,4,1024]{2,1,0:T(4,128)(2,1)S(1)} %bitcast.10) | data formatting | bytes 1048576
Async XLA Ops:
  0.0 9.1 %copy-start.6 = (s32[32,2]{0,1:T(2,128)S(1)}, s32[32,2]{0,1:T(2,128)}, u32[]{:S(2)}) copy-start(s32[32,2]{0,1:T(2,128)} %param.9) | copy-start | bytes 772
  0.0 19.6 %copy-start.5 = (bf16[256,256]{1,0:T(8,128)(2,1)S(1)}, bf16[256,256]{1,0:T(8,128)(2,1)}, u32[]{:S(2)}) copy-start(bf16[256,256]{1,0:T(8,128)(2,1)} %constant.10.clone.forward) | copy-start | bytes 393220
  2.0 17.7 %copy-start.1 = (bf16[256,256]{1,0:T(8,128)(2,1)S(1)}, bf16[256,256]{1,0:T(8,128)(2,1)}, u32[]{:S(2)}) copy-start(bf16[256,256]{1,0:T(8,128)(2,1)} %constant.14.clone.backward) | copy-start | bytes 393220
  2.0 17.7 %copy-start.2 = (bf16[256,256]{1,0:T(8,128)(2,1)S(1)}, bf16[256,256]{1,0:T(8,128)(2,1)}, u32[]{:S(2)}) copy-start(bf16[256,256]{1,0:T(8,128)(2,1)} %constant.13.clone.onward) | copy-start | bytes 393220
  2.0 17.7 %copy-start.3 = (bf16[256,256]{1,0:T(8,128)(2,1)S(1)}, bf16[256,256]{1,0:T(8,128)(2,1)}, u32[]{:S(2)}) copy-start(bf16[256,256]{1,0:T(8,128)(2,1)} %constant.12.clone.inverse_low) | copy-start | bytes 393220
  2.0 17.7 %copy-start.4 = (bf16[256,256]{1,0:T(8,128)(2,1)S(1)}, bf16[256,256]{1,0:T(8,128)(2,1)}, u32[]{:S(2)}) copy-start(bf16[256,256]{1,0:T(8,128)(2,1)} %constant.11.clone.inverse_high) | copy-start | bytes 393220
  2.0 17.7 %all-to-all-start = ((bf16[32,2,16,128]{3,2,1,0:T(8,128)(2,1)}), bf16[32,2,16,128]{3,2,1,0:T(8,128)(2,1)S(1)}, u32[]{:S(2)}, u32[]{:S(2)}) async-start(bf16[32,2,16,128]{3,2,1,0:T(8,128)(2,1)} %bitcast.2), calls=%async_computation | async-start | bytes 524288 | tf_op jit(solution)/shard_map/all_to_all | solution.py:273
  9.1 10.6 %copy-start = (f32[2,64]{1,0:T(2,128)S(1)}, f32[2,64]{1,0:T(2,128)}, u32[]{:S(2)}) copy-start(f32[2,64]{1,0:T(2,128)} %limits.1) | copy-start | bytes 1540
where the time goes:
time: 47.6 us; the launch traced here: 47.4 us
  blocking collectives  18.1 us (38%)
  waiting for transfers between devices  10.4 us (22%)
  Pallas kernels  8.83 us (19%)
  starting transfers between devices  7.1 us (15%)
  other arithmetic  1.96 us (4%)
  local copies, waits for them, and re-layouts  0.91 us (2%)
    all_to_all x1, blocking collectives, gathers_of_all_samples(): lax.all_to_all(restored, ('shot', 'tm'), split_axis=0, concat_axis=0, til...  18.1 us
    all_to_all x1, waiting for transfers between devices, gathers_of_all_samples(): lax.all_to_all(sent, ('shot', 'tm'), split_axis=0, concat_axis=0, tiled=T...  10.4 us
    pallas_call x1, Pallas kernels, gathers_of_all_samples(): pl.pallas_call(functools.partial(gather_kernel, shots), out_shape=jax.Sha...  8.83 us
    all_to_all x1, starting transfers between devices, gathers_of_all_samples(): lax.all_to_all(sent, ('shot', 'tm'), split_axis=0, concat_axis=0, tiled=T...  7.1 us
    convert_element_type x1, other arithmetic, gathers_of_all_samples(): sent = sent.astype(jnp.bfloat16).reshape(count, each, rows, BLK)  1.96 us
  transfers between devices with their start and end apart: 1, of which 1 were waited for; matrix products, arithmetic and copies ran while one was open for 0% of the time, Pallas kernels for 0%

commit v1 on v0

--- a/solution.py
+++ b/solution.py
@@ -20,6 +20,7 @@
 RELAX = 0.5
 HALF = WIN // 2
 SUB = 8
+SPAN = 4
 
 
 def split_table(table):
@@ -127,26 +128,22 @@
         return jnp.where(same, even, before), jnp.where(same, odd, even)
 
     def update(sweep):
-        def one(shot, carry):
-            for e in range(own):
-                first = (shot * own + e) * SRC_EXP
-                lags = [delays[shot * own + e, k] for k in range(SRC_EXP)]
-                for r in range(receivers):
-                    even, odd = record(r, shot, e)
+        for experiment in range(experiments):
+            shot, e = experiment // own, experiment % own
+            first = experiment * SRC_EXP
+            lags = [delays[experiment, k] for k in range(SRC_EXP)]
+            for r in range(receivers):
+                even, odd = record(r, shot, e)
+                if sweep > 0:
+                    estimate = [load(r, first + k) for k in range(SRC_EXP)]
+                    late = [delayed(*estimate[k], lags[k]) for k in range(SRC_EXP)]
+                    even = bfloat(even - sum(x[0] for x in late))
+                    odd = bfloat(odd - sum(x[1] for x in late))
+                for k in range(SRC_EXP):
+                    values = [RELAX * x for x in advanced(even, odd, lags[k])]
                     if sweep > 0:
-                        estimate = [load(r, first + k) for k in range(SRC_EXP)]
-                        late = [delayed(*estimate[k], lags[k]) for k in range(SRC_EXP)]
-                        even = bfloat(even - sum(x[0] for x in late))
-                        odd = bfloat(odd - sum(x[1] for x in late))
-                    for k in range(SRC_EXP):
-                        early = advanced(even, odd, lags[k])
-                        values = [RELAX * x for x in early]
-                        if sweep > 0:
-                            values = [a + b for a, b in zip(estimate[k], values)]
-                        store(r, first + k, values)
-            return carry
-
-        lax.fori_loop(0, shots, one, 0, unroll=2)
+                        values = [a + b for a, b in zip(estimate[k], values)]
+                    store(r, first + k, values)
 
     def columns(group, many=1):
         return slice(group * HALF, (group + many) * HALF)
@@ -154,10 +151,14 @@
     def forward_in_time():
         nyquist = jnp.zeros((sources, HALF), jnp.float32)
         for group in range(groups):
-            rows_of_group = slice(group * sources, (group + 1) * sources)
-            signal = jnp.concatenate([traces[half, rows_of_group, :] for half in range(2)], axis=1)
-            signal = signal.astype(jnp.bfloat16)
-            spectrum = product(signal, forward[...])
+            if group % SPAN == 0:
+                rows_of_span = slice(group * sources, (group + SPAN) * sources)
+                signal = jnp.concatenate(
+                    [traces[half, rows_of_span, :].astype(jnp.bfloat16) for half in range(2)],
+                    axis=1,
+                )
+                spectra = product(signal, forward[...])
+            spectrum = spectra[group % SPAN * sources : (group % SPAN + 1) * sources]
             real, imag = spectrum[:, :HALF], spectrum[:, HALF:]
             moved = pltpu.roll(imag, group, 1) if group else imag
             nyquist = jnp.where(lane_of_group == group, moved, nyquist)
@@ -215,11 +216,11 @@
                     back_low[rows_of_group, columns(half)] = low
                 group += 1
 
-    def back_in_time(rows_of_pair):
-        high = back_high[rows_of_pair, :]
+    def back_in_time(rows_of_span):
+        high = back_high[rows_of_span, :]
         return (
             product(high, inverse_high[...])
-            + product(back_low[rows_of_pair, :], inverse_high[...])
+            + product(back_low[rows_of_span, :], inverse_high[...])
             + product(high, inverse_low[...])
         )
 
@@ -249,14 +250,16 @@
         forward_in_time()
         shrink(sweep)
         back_in_source()
-        for group in range(0, groups, 2):
-            rows_of_pair = slice(group * sources, (group + 2) * sources)
-            restored = back_in_time(rows_of_pair)
+        for start in range(0, groups, SPAN):
+            rows_of_span = slice(start * sources, (start + SPAN) * sources)
+            restored = back_in_time(rows_of_span)
             if sweep < ITERS - 1:
                 for half in range(2):
-                    traces[half, rows_of_pair, :] = bfloat(restored[:, columns(half)])
-            else:
-                deliver(group // windows, group % windows, restored)
+                    traces[half, rows_of_span, :] = bfloat(restored[:, columns(half)])
+                continue
+            for group in range(0, SPAN, 2):
+                pair = restored[group * sources : (group + 2) * sources]
+                deliver((start + group) // windows, (start + group) % windows, pair)
 
 
 def gathers_of_all_samples(shots, blended, delays, thresholds):
@@ -269,7 +272,7 @@
     groups = each * windows
     rows = blocks * own
     sent = blended.reshape(receivers, own, blocks, BLK).transpose(0, 2, 1, 3)
-    sent = sent.astype(jnp.bfloat16).reshape(count, each, rows, BLK)
+    sent = lax.optimization_barrier(sent.reshape(count, each, rows, BLK)).astype(jnp.bfloat16)
     received = lax.all_to_all(sent, ("shot", "tm"), split_axis=0, concat_axis=0, tiled=True)
     tables = [jnp.asarray(table) for table in half_spectrum_tables()]
     vmem = pl.BlockSpec(memory_space=pltpu.VMEM)

time: 47.6 us -> 45 us (0.945)
  Pallas kernels: 8.83 us -> 6.37 us
    pallas_call x1, Pallas kernels: 8.83 us -> 6.37 us  [gathers_of_all_samples(): pl.pallas_call(functools.partial(gather_kernel, shots), out_shape=jax.Sha...]
where the time goes in v1:
time: 45 us; the launch traced here: 44.8 us
  blocking collectives  18.1 us (40%)
  waiting for transfers between devices  10.4 us (23%)
  starting transfers between devices  7.1 us (16%)
  Pallas kernels  6.37 us (14%)
  other arithmetic  1.82 us (4%)
  local copies, waits for them, and re-layouts  0.91 us (2%)
    all_to_all x1, blocking collectives, gathers_of_all_samples(): lax.all_to_all(restored, ('shot', 'tm'), split_axis=0, concat_axis=0, til...  18.1 us
    all_to_all x1, waiting for transfers between devices, gathers_of_all_samples(): lax.all_to_all(sent, ('shot', 'tm'), split_axis=0, concat_axis=0, tiled=T...  10.4 us
    all_to_all x1, starting transfers between devices, gathers_of_all_samples(): lax.all_to_all(sent, ('shot', 'tm'), split_axis=0, concat_axis=0, tiled=T...  7.1 us
    pallas_call x1, Pallas kernels, gathers_of_all_samples(): pl.pallas_call(functools.partial(gather_kernel, shots), out_shape=jax.Sha...  6.37 us
    convert_element_type x1, other arithmetic, gathers_of_all_samples(): lax.optimization_barrier(sent.reshape(count, each, rows, BLK))  1.82 us
    unnamed x16, local copies, waits for them, and re-layouts  0.91 us
  transfers between devices with their start and end apart: 1, of which 1 were waited for; matrix products, arithmetic and copies ran while one was open for 0% of the time, Pallas kernels for 0%

profile of v1, /device:TPU:1, one launch (start us, length us, event | category | flops | bytes accessed | tf_op | source)
XLA Modules:
  0.0 44.8 jit_solution(9965130985913098668)
XLA Ops:
  0.0 0.0 copy-start.6
  0.0 0.0 copy-start.5
  0.0 1.8 %convert_element_type.3 = bf16[32,2,16,128]{3,2,1,0:T(8,128)(2,1)} convert(f32[32,2,16,128]{3,2,1,0:T(8,128)} %bitcast.11) | non-fusion elementwise | flops 131072 | bytes 786432 | tf_op jit(solution)/shard_map/convert_element_type | solution.py:275
  1.8 0.0 copy-start.1
  1.8 0.0 copy-start.2
  1.8 0.0 copy-start.3
  1.8 0.0 copy-start.4
  1.8 7.1 %all-to-all-start = ((bf16[32,2,16,128]{3,2,1,0:T(8,128)(2,1)}), bf16[32,2,16,128]{3,2,1,0:T(8,128)(2,1)S(1)}, u32[]{:S(2)}, u32[]{:S(2)}) async-start(bf16[32,2,16,128]{3,2,1,0:T(8,128)(2,1)} %convert_element_type.3), calls=%async_computation | async-start | bytes 524288 | tf_op jit(solution)/shard_map/all_to_all | solution.py:276
  8.9 0.0 copy-done.6
  9.0 0.0 copy-start
  9.0 0.1 copy.10.delays
  9.1 10.4 %all-to-all-done.received = bf16[32,2,16,128]{3,2,1,0:T(8,128)(2,1)S(1)} async-done(((bf16[32,2,16,128]{3,2,1,0:T(8,128)(2,1)}), bf16[32,2,16,128]{3,2,1,0:T(8,128)(2,1)S(1)}, u32[]{:S(2)}, u32[]{:S(2)}) %all-to-all-start) | async-done | bytes 262176 | tf_op jit(solution)/shard_map/all_to_all | solution.py:276
  19.5 0.0 copy-done.5
  19.5 0.0 copy-done.1
  19.5 0.0 copy-done.2
  19.5 0.0 copy-done.3
  19.5 0.0 copy-done.4
  19.5 0.0 copy-done
  19.5 6.4 %shard_map.82 = bf16[32,2,32,128]{3,2,1,0:T(8,128)(2,1)S(1)} custom-call(s32[32,2]{1,0:T(8,128)S(1)} %copy.10.delays, f32[2,64]{1,0:T(2,128)S(1)} %copy-done, bf16[32,2,16,128]{3,2,1,0:T(8,128)(2,1)S(1)} %all-to-all-done.received, bf16[256,256]{1,0:T(8,128)(2,1)S(1)} %copy-done.5, bf16[256,256]{1,0:T(8,128)(2,1)S(1)} %copy-done.4, ...), custom_call_target="tpu_custom_call" | custom-call | flops 2415919104 | bytes 2097152 | tf_op jit(solution)/shard_map/pallas_call | solution.py:280
  25.9 18.1 %all_to_all.10 = bf16[32,2,32,128]{3,2,1,0:T(8,128)(2,1)S(1)} all-to-all(bf16[32,2,32,128]{3,2,1,0:T(8,128)(2,1)S(1)} %shard_map.82), channel_id=1, replica_groups=mesh['shot'=16,'tm'=2] {'shot','tm'}, dimensions={0} | all-to-all | bytes 1048576 | tf_op jit(solution)/shard_map/all_to_all | solution.py:300
  44.0 0.8 %copy.13 = bf16[64,4,1024]{2,1,0:T(4,128)(2,1)} copy(bf16[64,4,1024]{2,1,0:T(4,128)(2,1)S(1)} %bitcast.10) | data formatting | bytes 1048576
Async XLA Ops:
  0.0 8.9 %copy-start.6 = (s32[32,2]{0,1:T(2,128)S(1)}, s32[32,2]{0,1:T(2,128)}, u32[]{:S(2)}) copy-start(s32[32,2]{0,1:T(2,128)} %param.9) | copy-start | bytes 772
  0.0 19.5 %copy-start.5 = (bf16[256,256]{1,0:T(8,128)(2,1)S(1)}, bf16[256,256]{1,0:T(8,128)(2,1)}, u32[]{:S(2)}) copy-start(bf16[256,256]{1,0:T(8,128)(2,1)} %constant.10.clone.forward) | copy-start | bytes 393220
  1.8 17.7 %copy-start.1 = (bf16[256,256]{1,0:T(8,128)(2,1)S(1)}, bf16[256,256]{1,0:T(8,128)(2,1)}, u32[]{:S(2)}) copy-start(bf16[256,256]{1,0:T(8,128)(2,1)} %constant.14.clone.backward) | copy-start | bytes 393220
  1.8 17.7 %copy-start.2 = (bf16[256,256]{1,0:T(8,128)(2,1)S(1)}, bf16[256,256]{1,0:T(8,128)(2,1)}, u32[]{:S(2)}) copy-start(bf16[256,256]{1,0:T(8,128)(2,1)} %constant.13.clone.onward) | copy-start | bytes 393220
  1.8 17.7 %copy-start.3 = (bf16[256,256]{1,0:T(8,128)(2,1)S(1)}, bf16[256,256]{1,0:T(8,128)(2,1)}, u32[]{:S(2)}) copy-start(bf16[256,256]{1,0:T(8,128)(2,1)} %constant.12.clone.inverse_low) | copy-start | bytes 393220
  1.8 17.7 %copy-start.4 = (bf16[256,256]{1,0:T(8,128)(2,1)S(1)}, bf16[256,256]{1,0:T(8,128)(2,1)}, u32[]{:S(2)}) copy-start(bf16[256,256]{1,0:T(8,128)(2,1)} %constant.11.clone.inverse_high) | copy-start | bytes 393220
  1.8 17.7 %all-to-all-start = ((bf16[32,2,16,128]{3,2,1,0:T(8,128)(2,1)}), bf16[32,2,16,128]{3,2,1,0:T(8,128)(2,1)S(1)}, u32[]{:S(2)}, u32[]{:S(2)}) async-start(bf16[32,2,16,128]{3,2,1,0:T(8,128)(2,1)} %convert_element_type.3), calls=%async_computation | async-start | bytes 524288 | tf_op jit(solution)/shard_map/all_to_all | solution.py:276
  9.0 10.6 %copy-start = (f32[2,64]{1,0:T(2,128)S(1)}, f32[2,64]{1,0:T(2,128)}, u32[]{:S(2)}) copy-start(f32[2,64]{1,0:T(2,128)} %limits.1) | copy-start | bytes 1540

commit v2 on v1

--- a/solution.py
+++ b/solution.py
@@ -269,35 +269,41 @@
     each = receivers // count
     blocks = samples // BLK
     windows = samples * blocks_of_time // WIN
-    groups = each * windows
     rows = blocks * own
     sent = blended.reshape(receivers, own, blocks, BLK).transpose(0, 2, 1, 3)
-    sent = lax.optimization_barrier(sent.reshape(count, each, rows, BLK)).astype(jnp.bfloat16)
-    received = lax.all_to_all(sent, ("shot", "tm"), split_axis=0, concat_axis=0, tiled=True)
+    sent = lax.optimization_barrier(sent.reshape(each, count, rows, BLK))
+
+    def exchanged(array):
+        return lax.all_to_all(array, ("shot", "tm"), split_axis=0, concat_axis=0, tiled=True)
+
     tables = [jnp.asarray(table) for table in half_spectrum_tables()]
     vmem = pl.BlockSpec(memory_space=pltpu.VMEM)
     held = SRC // shots
-    restored = pl.pallas_call(
+    filtered = pl.pallas_call(
         functools.partial(gather_kernel, shots),
-        out_shape=jax.ShapeDtypeStruct((count, each, blocks * held, BLK), jnp.bfloat16),
+        out_shape=jax.ShapeDtypeStruct((count, 1, blocks * held, BLK), jnp.bfloat16),
         in_specs=[pl.BlockSpec(memory_space=pltpu.SMEM)] + [vmem] * 7,
         out_specs=vmem,
         scratch_shapes=[
-            pltpu.VMEM((each, shots, blocks_of_time * rows, BLK), jnp.float32),
-            pltpu.VMEM((4 * SRC, (groups + 1) * HALF), jnp.bfloat16),
-            pltpu.VMEM((4 * SRC, (groups + 1) * HALF), jnp.bfloat16),
-            pltpu.VMEM((groups * SRC, WIN), jnp.bfloat16),
-            pltpu.VMEM((groups * SRC, WIN), jnp.bfloat16),
-            pltpu.VMEM((2, groups * SRC, BLK), jnp.float32),
+            pltpu.VMEM((1, shots, blocks_of_time * rows, BLK), jnp.float32),
+            pltpu.VMEM((4 * SRC, (windows + 1) * HALF), jnp.bfloat16),
+            pltpu.VMEM((4 * SRC, (windows + 1) * HALF), jnp.bfloat16),
+            pltpu.VMEM((windows * SRC, WIN), jnp.bfloat16),
+            pltpu.VMEM((windows * SRC, WIN), jnp.bfloat16),
+            pltpu.VMEM((2, windows * SRC, BLK), jnp.float32),
         ],
-        compiler_params=pltpu.CompilerParams(vmem_limit_bytes=40 * 1024 * 1024),
+        compiler_params=pltpu.CompilerParams(vmem_limit_bytes=24 * 1024 * 1024),
         cost_estimate=pl.CostEstimate(
-            flops=2 * ITERS * groups * SRC * WIN * WIN * 9,
+            flops=2 * ITERS * windows * SRC * WIN * WIN * 9,
             bytes_accessed=2 * 1024 * 1024,
-            transcendentals=ITERS * groups * SRC * HALF,
+            transcendentals=ITERS * windows * SRC * HALF,
         ),
-    )(delays, thresholds, received, *tables)
-    final = lax.all_to_all(restored, ("shot", "tm"), split_axis=0, concat_axis=0, tiled=True)
+    )
+    received = [exchanged(sent[half].astype(jnp.bfloat16)) for half in range(each)]
+    restored = [
+        exchanged(filtered(delays, thresholds, part[:, None], *tables)) for part in received
+    ]
+    final = jnp.concatenate(restored, axis=0)
     final = final.reshape(receivers, blocks, held, BLK).transpose(0, 2, 1, 3)
     return final.reshape(receivers, held, samples)
 

time: 45 us -> 56.6 us (1.26)
  blocking collectives: 18.1 us -> 27.6 us
  Pallas kernels: 6.37 us -> 9.54 us
  waiting for transfers between devices: 10.4 us -> 8.29 us
    all_to_all x1 -> x2, blocking collectives: 18.1 us -> 27.6 us  [exchanged(): lax.all_to_all(array, ('shot', 'tm'), split_axis=0, concat_axis=0, tiled=...]
    pallas_call x1 -> x2, Pallas kernels: 6.37 us -> 9.54 us  [gathers_of_all_samples(): filtered(delays, thresholds, part[:, None], *tables)]
    all_to_all x1 -> x2, waiting for transfers between devices: 10.4 us -> 8.29 us  [exchanged(): lax.all_to_all(array, ('shot', 'tm'), split_axis=0, concat_axis=0, tiled=...]
    convert_element_type x1 -> x0, other arithmetic: 1.82 us -> none  [gathers_of_all_samples(): lax.optimization_barrier(sent.reshape(count, each, rows, BLK))]
    another operation x0 -> x1, other arithmetic: none -> 1.08 us
    concatenate x0 -> x1, other arithmetic: none -> 0.84 us  [gathers_of_all_samples(): final = jnp.concatenate(restored, axis=0)]
    convert_element_type x0 -> x1, local copies, waits for them, and re-layouts: none -> 0.65 us  [gathers_of_all_samples(): sent[half].astype(jnp.bfloat16)]
    all_to_all x1 -> x2, starting transfers between devices: 7.1 us -> 7.05 us  [exchanged(): lax.all_to_all(array, ('shot', 'tm'), split_axis=0, concat_axis=0, tiled=...]
  transfers between devices with their start and end apart: 1 -> 2, of which waited for: 1 -> 2; matrix products, arithmetic and copies ran while one was open for 0% -> 0% of each run, Pallas kernels for 0% -> 17%
where the time goes in v2:
time: 56.6 us; the launch traced here: 55.9 us
  blocking collectives  27.6 us (49%)
  Pallas kernels  9.54 us (17%)
  waiting for transfers between devices  8.29 us (15%)
  starting transfers between devices  7.05 us (12%)
  other arithmetic  1.92 us (3%)
  local copies, waits for them, and re-layouts  1.41 us (2%)
    all_to_all x2, blocking collectives, exchanged(): lax.all_to_all(array, ('shot', 'tm'), split_axis=0, concat_axis=0, tiled=...  27.6 us
    pallas_call x2, Pallas kernels, gathers_of_all_samples(): filtered(delays, thresholds, part[:, None], *tables)  9.54 us
    all_to_all x2, waiting for transfers between devices, exchanged(): lax.all_to_all(array, ('shot', 'tm'), split_axis=0, concat_axis=0, tiled=...  8.29 us
    all_to_all x2, starting transfers between devices, exchanged(): lax.all_to_all(array, ('shot', 'tm'), split_axis=0, concat_axis=0, tiled=...  7.05 us
  transfers between devices with their start and end apart: 2, of which 2 were waited for; matrix products, arithmetic and copies ran while one was open for 0% of the time, Pallas kernels for 17%

profile of v2, /device:TPU:1, one launch (start us, length us, event | category | flops | bytes accessed | tf_op | source)
XLA Modules:
  0.0 55.9 jit_solution(5351479151868023857)
XLA Ops:
  0.0 1.1 %convert.4 = bf16[2,32,16,128]{3,2,1,0:T(8,128)(2,1)S(1)} convert(f32[2,32,16,128]{3,2,1,0:T(8,128)} %bitcast.20) | non-fusion elementwise | flops 131072 | bytes 786432 | tf_op jit(solution)/shard_map/convert.1
  1.1 0.0 copy-start.5
  1.1 0.7 %slice_bitcast_fusion.1 = (bf16[32,16,128]{2,1,0:T(8,128)(2,1)}, bf16[32,16,128]{2,1,0:T(8,128)(2,1)S(1)}) fusion(bf16[2,32,16,128]{3,2,1,0:T(8,128)(2,1)S(1)} %convert.4), kind=kLoop, calls=%fused_computation.2 | loop fusion | bytes 524288 | tf_op jit(solution)/shard_map/convert_element_type | solution.py:302
  1.7 0.0 copy-start.6
  1.8 0.0 copy-start.3
  1.8 0.0 copy-start.4
  1.8 14.8 %all_to_all.20 = bf16[32,16,128]{2,1,0:T(8,128)(2,1)S(1)} all-to-all(bf16[32,16,128]{2,1,0:T(8,128)(2,1)S(1)} %get-tuple-element.6), channel_id=1, replica_groups=mesh['shot'=16,'tm'=2] {'shot','tm'}, dimensions={0} | all-to-all | bytes 262144 | tf_op jit(solution)/shard_map/all_to_all | solution.py:277
  16.6 0.0 copy-start.1
  16.6 0.0 copy-start.2
  16.6 3.2 %all-to-all-start = ((bf16[32,16,128]{2,1,0:T(8,128)(2,1)}), bf16[32,16,128]{2,1,0:T(8,128)(2,1)S(1)}, u32[]{:S(2)}, u32[]{:S(2)}) async-start(bf16[32,16,128]{2,1,0:T(8,128)(2,1)} %get-tuple-element.5), calls=%async_computation | async-start | bytes 262144 | tf_op jit(solution)/shard_map/all_to_all | solution.py:277
  19.8 0.0 copy-done.6
  19.8 0.1 copy.10.delays
  19.9 0.0 copy-start
  19.9 0.0 copy-done.5
  19.9 0.0 copy-done.3
  19.9 0.0 copy-done.4
  20.0 0.0 copy-done.1
  20.0 0.0 copy-done.2
  20.0 0.6 %copy-done = f32[2,64]{1,0:T(2,128)S(1)} copy-done((f32[2,64]{1,0:T(2,128)S(1)}, f32[2,64]{1,0:T(2,128)}, u32[]{:S(2)}) %copy-start) | copy-done | bytes 536
  20.6 5.1 %shard_map.83 = bf16[32,1,32,128]{3,2,1,0:T(8,128)(2,1)} custom-call(s32[32,2]{1,0:T(8,128)S(1)} %copy.10.delays, f32[2,64]{1,0:T(2,128)S(1)} %copy-done, bf16[32,1,16,128]{3,2,1,0:T(8,128)(2,1)S(1)} %bitcast.19, bf16[256,256]{1,0:T(8,128)(2,1)S(1)} %copy-done.5, bf16[256,256]{1,0:T(8,128)(2,1)S(1)} %copy-done.4, bf16[256,256]{1,0:T(8,128)(2,1)S(1)} %copy-done.3, ...), custom_call_target="tpu_custom_call" | custom-call | flops 1207959552 | bytes 2097152 | tf_op jit(solution)/shard_map/pallas_call | solution.py:304
  25.7 2.2 %all-to-all-done = bf16[32,16,128]{2,1,0:T(8,128)(2,1)S(1)} async-done(((bf16[32,16,128]{2,1,0:T(8,128)(2,1)}), bf16[32,16,128]{2,1,0:T(8,128)(2,1)S(1)}, u32[]{:S(2)}, u32[]{:S(2)}) %all-to-all-start) | async-done | bytes 131104 | tf_op jit(solution)/shard_map/all_to_all | solution.py:277
  27.9 3.8 %all-to-all-start.3 = ((bf16[32,1,32,128]{3,2,1,0:T(8,128)(2,1)}), bf16[32,1,32,128]{3,2,1,0:T(8,128)(2,1)S(1)}, u32[]{:S(2)}, u32[]{:S(2)}) async-start(bf16[32,1,32,128]{3,2,1,0:T(8,128)(2,1)} %shard_map.83), calls=%async_computation.3 | async-start | bytes 524288 | tf_op jit(solution)/shard_map/all_to_all | solution.py:277
  31.7 4.4 %shard_map.82 = bf16[32,1,32,128]{3,2,1,0:T(8,128)(2,1)S(1)} custom-call(s32[32,2]{1,0:T(8,128)S(1)} %copy.10.delays, f32[2,64]{1,0:T(2,128)S(1)} %copy-done, bf16[32,1,16,128]{3,2,1,0:T(8,128)(2,1)S(1)} %bitcast.18, bf16[256,256]{1,0:T(8,128)(2,1)S(1)} %copy-done.5, bf16[256,256]{1,0:T(8,128)(2,1)S(1)} %copy-done.4, bf16[256,256]{1,0:T(8,128)(2,1)S(1)} %copy-done.3, ...), custom_call_target="tpu_custom_call" | custom-call | flops 1207959552 | bytes 2097152 | tf_op jit(solution)/shard_map/pallas_call | solution.py:304
  36.1 6.1 %all-to-all-done.3 = bf16[32,1,32,128]{3,2,1,0:T(8,128)(2,1)S(1)} async-done(((bf16[32,1,32,128]{3,2,1,0:T(8,128)(2,1)}), bf16[32,1,32,128]{3,2,1,0:T(8,128)(2,1)S(1)}, u32[]{:S(2)}, u32[]{:S(2)}) %all-to-all-start.3) | async-done | bytes 262176 | tf_op jit(solution)/shard_map/all_to_all | solution.py:277
  42.3 12.8 %all_to_all.21 = bf16[32,1,32,128]{3,2,1,0:T(8,128)(2,1)S(1)} all-to-all(bf16[32,1,32,128]{3,2,1,0:T(8,128)(2,1)S(1)} %shard_map.82), channel_id=1, replica_groups=mesh['shot'=16,'tm'=2] {'shot','tm'}, dimensions={0} | all-to-all | bytes 524288 | tf_op jit(solution)/shard_map/all_to_all | solution.py:277
  55.1 0.8 %pad_maximum_fusion = bf16[64,1,32,128]{3,2,1,0:T(8,128)(2,1)} fusion(bf16[32,1,32,128]{3,2,1,0:T(8,128)(2,1)S(1)} %all-to-all-done.3, bf16[32,1,32,128]{3,2,1,0:T(8,128)(2,1)S(1)} %all_to_all.21), kind=kLoop, calls=%fused_computation | loop fusion | flops 262144 | bytes 1048576 | tf_op jit(solution)/shard_map/concatenate | solution.py:306
Async XLA Ops:
  1.1 18.9 %copy-start.5 = (bf16[256,256]{1,0:T(8,128)(2,1)S(1)}, bf16[256,256]{1,0:T(8,128)(2,1)}, u32[]{:S(2)}) copy-start(bf16[256,256]{1,0:T(8,128)(2,1)} %constant.10.clone.forward) | copy-start | bytes 393220
  1.7 18.1 %copy-start.6 = (s32[32,2]{0,1:T(2,128)S(1)}, s32[32,2]{0,1:T(2,128)}, u32[]{:S(2)}) copy-start(s32[32,2]{0,1:T(2,128)} %param.9) | copy-start | bytes 772
  1.8 18.2 %copy-start.3 = (bf16[256,256]{1,0:T(8,128)(2,1)S(1)}, bf16[256,256]{1,0:T(8,128)(2,1)}, u32[]{:S(2)}) copy-start(bf16[256,256]{1,0:T(8,128)(2,1)} %constant.12.clone.inverse_low) | copy-start | bytes 393220
  1.8 18.2 %copy-start.4 = (bf16[256,256]{1,0:T(8,128)(2,1)S(1)}, bf16[256,256]{1,0:T(8,128)(2,1)}, u32[]{:S(2)}) copy-start(bf16[256,256]{1,0:T(8,128)(2,1)} %constant.11.clone.inverse_high) | copy-start | bytes 393220
  16.6 3.4 %copy-start.1 = (bf16[256,256]{1,0:T(8,128)(2,1)S(1)}, bf16[256,256]{1,0:T(8,128)(2,1)}, u32[]{:S(2)}) copy-start(bf16[256,256]{1,0:T(8,128)(2,1)} %constant.14.clone.backward) | copy-start | bytes 393220
  16.6 3.4 %copy-start.2 = (bf16[256,256]{1,0:T(8,128)(2,1)S(1)}, bf16[256,256]{1,0:T(8,128)(2,1)}, u32[]{:S(2)}) copy-start(bf16[256,256]{1,0:T(8,128)(2,1)} %constant.13.clone.onward) | copy-start | bytes 393220
  16.6 11.3 %all-to-all-start = ((bf16[32,16,128]{2,1,0:T(8,128)(2,1)}), bf16[32,16,128]{2,1,0:T(8,128)(2,1)S(1)}, u32[]{:S(2)}, u32[]{:S(2)}) async-start(bf16[32,16,128]{2,1,0:T(8,128)(2,1)} %get-tuple-element.5), calls=%async_computation | async-start | bytes 262144 | tf_op jit(solution)/shard_map/all_to_all | solution.py:277
  19.9 0.7 %copy-start = (f32[2,64]{1,0:T(2,128)S(1)}, f32[2,64]{1,0:T(2,128)}, u32[]{:S(2)}) copy-start(f32[2,64]{1,0:T(2,128)} %limits.3) | copy-start | bytes 1540
  27.9 14.4 %all-to-all-start.3 = ((bf16[32,1,32,128]{3,2,1,0:T(8,128)(2,1)}), bf16[32,1,32,128]{3,2,1,0:T(8,128)(2,1)S(1)}, u32[]{:S(2)}, u32[]{:S(2)}) async-start(bf16[32,1,32,128]{3,2,1,0:T(8,128)(2,1)} %shard_map.83), calls=%async_computation.3 | async-start | bytes 524288 | tf_op jit(solution)/shard_map/all_to_all | solution.py:277

commit v3 on v1

--- a/solution.py
+++ b/solution.py
@@ -21,6 +21,7 @@
 HALF = WIN // 2
 SUB = 8
 SPAN = 4
+TILE = 256
 
 
 def split_table(table):
@@ -50,6 +51,20 @@
     return (forward, *split_table(inverse), *pair)
 
 
+def rearranging(shape, axes):
+    order = np.arange(math.prod(shape)).reshape(shape).transpose(axes).reshape(-1)
+    return np.eye(order.size)[order].astype(ml_dtypes.bfloat16)
+
+
+def order_tables(windows, own):
+    shots, sources = TILE // (2 * windows * own), TILE // windows
+    return (
+        rearranging((shots, windows, 2, own), (0, 3, 2, 1)),
+        rearranging((sources, windows), (1, 0)),
+        rearranging((windows, sources), (1, 0)),
+    )
+
+
 def halves(value):
     high = value.astype(jnp.bfloat16)
     return high, (value - high.astype(jnp.float32)).astype(jnp.bfloat16)
@@ -73,46 +88,33 @@
     inverse_low,
     onward,
     backward,
+    order_arrived,
+    order_windows,
+    order_sources,
     out,
     records,
     field,
     mixed,
     back_high,
     back_low,
-    traces,
+    estimates,
 ):
     count, receivers, rows, _ = received.shape
     blocks_of_time = count // shots
-    experiments, sources = delays.shape[0], SRC
-    own = experiments // shots
-    windows = records.shape[2] // (2 * own)
+    experiments, sources = delays.shape[1], SRC
+    windows = blocks_of_time * rows * shots // (2 * experiments)
     groups = receivers * windows
     parts = windows // blocks_of_time
+    some = TILE // windows
     lane = lax.broadcasted_iota(jnp.int32, (windows, BLK), 1)
     row = lax.broadcasted_iota(jnp.int32, (windows, BLK), 0)
     lane_of_group = lax.broadcasted_iota(jnp.int32, (sources, HALF), 1)
-
-    for shot in range(shots):
-        for block in range(blocks_of_time):
-            arrived = received[shot * blocks_of_time + block].astype(jnp.float32)
-            for r in range(receivers):
-                records[r, shot, block * rows : (block + 1) * rows, :] = arrived[r]
-
-    def record(r, shot, e):
-        return tuple(
-            records[r, shot, pl.ds(half * own + e, windows, stride=2 * own), :]
-            for half in range(2)
-        )
-
-    def trace_rows(r, s):
-        return pl.ds(r * windows * sources + s, windows, stride=sources)
-
-    def load(r, s):
-        return tuple(traces[half, trace_rows(r, s), :] for half in range(2))
-
-    def store(r, s, values):
-        for half in range(2):
-            traces[half, trace_rows(r, s), :] = values[half]
+    lane_of_some = lax.broadcasted_iota(jnp.int32, (some, HALF), 1)
+
+    for chunk in range(sources // some):
+        senders = slice(chunk * TILE // rows, (chunk + 1) * TILE // rows)
+        arrived = [received[senders, r].reshape(TILE, BLK) for r in range(receivers)]
+        records[chunk] = product(order_arrived[...], jnp.concatenate(arrived, axis=1))
 
     def advanced(even, odd, delay):
         by = (BLK - delay) & (BLK - 1)
@@ -127,50 +129,64 @@
         same = lane >= delay
         return jnp.where(same, even, before), jnp.where(same, odd, even)
 
-    def update(sweep):
-        for experiment in range(experiments):
-            shot, e = experiment // own, experiment % own
-            first = experiment * SRC_EXP
-            lags = [delays[experiment, k] for k in range(SRC_EXP)]
-            for r in range(receivers):
-                even, odd = record(r, shot, e)
-                if sweep > 0:
-                    estimate = [load(r, first + k) for k in range(SRC_EXP)]
-                    late = [delayed(*estimate[k], lags[k]) for k in range(SRC_EXP)]
-                    even = bfloat(even - sum(x[0] for x in late))
-                    odd = bfloat(odd - sum(x[1] for x in late))
-                for k in range(SRC_EXP):
-                    values = [RELAX * x for x in advanced(even, odd, lags[k])]
-                    if sweep > 0:
-                        values = [a + b for a, b in zip(estimate[k], values)]
-                    store(r, first + k, values)
-
     def columns(group, many=1):
         return slice(group * HALF, (group + many) * HALF)
 
-    def forward_in_time():
-        nyquist = jnp.zeros((sources, HALF), jnp.float32)
-        for group in range(groups):
-            if group % SPAN == 0:
-                rows_of_span = slice(group * sources, (group + SPAN) * sources)
-                signal = jnp.concatenate(
-                    [traces[half, rows_of_span, :].astype(jnp.bfloat16) for half in range(2)],
-                    axis=1,
-                )
-                spectra = product(signal, forward[...])
-            spectrum = spectra[group % SPAN * sources : (group % SPAN + 1) * sources]
-            real, imag = spectrum[:, :HALF], spectrum[:, HALF:]
-            moved = pltpu.roll(imag, group, 1) if group else imag
-            nyquist = jnp.where(lane_of_group == group, moved, nyquist)
-            imag = jnp.where(lane_of_group == 0, 0.0, imag)
-            put(field, columns(group), real, imag)
-        put(field, columns(groups), nyquist, jnp.zeros_like(nyquist))
-
-    def put(ref, where, real, imag):
+    def update(sweep, r, chunk):
+        if sweep > 0:
+            before = [
+                estimates[pl.ds((r * windows + w) * sources + chunk * some, some), :]
+                for w in range(windows)
+            ]
+            before = product(order_sources[...], jnp.concatenate(before, axis=0))
+        updated = []
+        for at in range(0, some, SRC_EXP):
+            experiment = (chunk * some + at) // SRC_EXP
+            lags = [delays[k, experiment] for k in range(SRC_EXP)]
+            even, odd = (
+                records[chunk, pl.ds((at + half) * windows, windows), columns(r)]
+                for half in range(2)
+            )
+            if sweep > 0:
+                estimate = [
+                    tuple(
+                        before[(at + k) * windows : (at + k + 1) * windows, columns(half)]
+                        for half in range(2)
+                    )
+                    for k in range(SRC_EXP)
+                ]
+                late = [delayed(*estimate[k], lags[k]) for k in range(SRC_EXP)]
+                even = bfloat(even - sum(x[0] for x in late))
+                odd = bfloat(odd - sum(x[1] for x in late))
+            for k in range(SRC_EXP):
+                values = [RELAX * x for x in advanced(even, odd, lags[k])]
+                if sweep > 0:
+                    values = [a + b for a, b in zip(estimate[k], values)]
+                updated.append(jnp.concatenate(values, axis=1))
+        return jnp.concatenate(updated, axis=0).astype(jnp.bfloat16)
+
+    def update_and_forward_in_time(sweep):
+        for chunk in range(sources // some):
+            nyquist = jnp.zeros((some, HALF), jnp.float32)
+            for r in range(receivers):
+                signal = product(order_windows[...], update(sweep, r, chunk))
+                spectra = product(signal.astype(jnp.bfloat16), forward[...])
+                for w in range(windows):
+                    group = r * windows + w
+                    spectrum = spectra[w * some : (w + 1) * some]
+                    real, imag = spectrum[:, :HALF], spectrum[:, HALF:]
+                    moved = pltpu.roll(imag, group, 1) if group else imag
+                    nyquist = jnp.where(lane_of_some == group, moved, nyquist)
+                    imag = jnp.where(lane_of_some == 0, 0.0, imag)
+                    put(field, columns(group), real, imag, chunk * some)
+            put(field, columns(groups), nyquist, jnp.zeros_like(nyquist), chunk * some)
+
+    def put(ref, where, real, imag, first=0):
         real_high, real_low = halves(real)
         imag_high, imag_low = halves(imag)
         for at, value in enumerate((real_high, imag_high, real_low, imag_low)):
-            ref[at * sources : (at + 1) * sources, where] = value
+            start = at * sources + first
+            ref[start : start + value.shape[0], where] = value
 
     def chunks():
         yield columns(groups)
@@ -246,16 +262,14 @@
                 out[target, r, inside * SUB : (inside + 2) * SUB, :] = both[k]
 
     for sweep in range(ITERS):
-        update(sweep)
-        forward_in_time()
+        update_and_forward_in_time(sweep)
         shrink(sweep)
         back_in_source()
         for start in range(0, groups, SPAN):
             rows_of_span = slice(start * sources, (start + SPAN) * sources)
             restored = back_in_time(rows_of_span)
             if sweep < ITERS - 1:
-                for half in range(2):
-                    traces[half, rows_of_span, :] = bfloat(restored[:, columns(half)])
+                estimates[rows_of_span, :] = restored.astype(jnp.bfloat16)
                 continue
             for group in range(0, SPAN, 2):
                 pair = restored[group * sources : (group + 2) * sources]
@@ -274,21 +288,22 @@
     sent = blended.reshape(receivers, own, blocks, BLK).transpose(0, 2, 1, 3)
     sent = lax.optimization_barrier(sent.reshape(count, each, rows, BLK)).astype(jnp.bfloat16)
     received = lax.all_to_all(sent, ("shot", "tm"), split_axis=0, concat_axis=0, tiled=True)
-    tables = [jnp.asarray(table) for table in half_spectrum_tables()]
+    tables = half_spectrum_tables() + order_tables(windows, own)
+    tables = [jnp.asarray(table) for table in tables]
     vmem = pl.BlockSpec(memory_space=pltpu.VMEM)
     held = SRC // shots
     restored = pl.pallas_call(
         functools.partial(gather_kernel, shots),
         out_shape=jax.ShapeDtypeStruct((count, each, blocks * held, BLK), jnp.bfloat16),
-        in_specs=[pl.BlockSpec(memory_space=pltpu.SMEM)] + [vmem] * 7,
+        in_specs=[pl.BlockSpec(memory_space=pltpu.SMEM)] + [vmem] * (2 + len(tables)),
         out_specs=vmem,
         scratch_shapes=[
-            pltpu.VMEM((each, shots, blocks_of_time * rows, BLK), jnp.float32),
+            pltpu.VMEM((SRC * windows // TILE, TILE, each * BLK), jnp.float32),
             pltpu.VMEM((4 * SRC, (groups + 1) * HALF), jnp.bfloat16),
             pltpu.VMEM((4 * SRC, (groups + 1) * HALF), jnp.bfloat16),
             pltpu.VMEM((groups * SRC, WIN), jnp.bfloat16),
             pltpu.VMEM((groups * SRC, WIN), jnp.bfloat16),
-            pltpu.VMEM((2, groups * SRC, BLK), jnp.float32),
+            pltpu.VMEM((groups * SRC, WIN), jnp.bfloat16),
         ],
         compiler_params=pltpu.CompilerParams(vmem_limit_bytes=40 * 1024 * 1024),
         cost_estimate=pl.CostEstimate(
@@ -296,7 +311,7 @@
             bytes_accessed=2 * 1024 * 1024,
             transcendentals=ITERS * groups * SRC * HALF,
         ),
-    )(delays, thresholds, received, *tables)
+    )(delays.T, thresholds, received, *tables)
     final = lax.all_to_all(restored, ("shot", "tm"), split_axis=0, concat_axis=0, tiled=True)
     final = final.reshape(receivers, blocks, held, BLK).transpose(0, 2, 1, 3)
     return final.reshape(receivers, held, samples)

time: 45 us -> 44.3 us (0.984)
  blocking collectives: 18.1 us -> 35.5 us
  waiting for transfers between devices: 10.4 us -> 0 us
  starting transfers between devices: 7.1 us -> 0 us
  other arithmetic: 1.82 us -> 1.14 us
  local copies, waits for them, and re-layouts: 0.91 us -> 1.45 us
  Pallas kernels: 6.37 us -> 5.89 us
    all_to_all x0 -> x1, blocking collectives: none -> 17.5 us  [gathers_of_all_samples(): lax.all_to_all(sent, ('shot', 'tm'), split_axis=0, concat_axis=0, tiled=T...]
    all_to_all x1 -> x0, waiting for transfers between devices: 10.4 us -> none  [gathers_of_all_samples(): lax.all_to_all(sent, ('shot', 'tm'), split_axis=0, concat_axis=0, tiled=T...]
    all_to_all x1 -> x0, starting transfers between devices: 7.1 us -> none  [gathers_of_all_samples(): lax.all_to_all(sent, ('shot', 'tm'), split_axis=0, concat_axis=0, tiled=T...]
    convert_element_type x1, other arithmetic: 1.82 us -> 1.14 us  [gathers_of_all_samples(): lax.optimization_barrier(sent.reshape(count, each, rows, BLK))]
    unnamed x16 -> x21, local copies, waits for them, and re-layouts: 0.91 us -> 1.45 us
    pallas_call x1, Pallas kernels: 6.37 us -> 5.89 us  [gathers_of_all_samples(): pl.pallas_call(functools.partial(gather_kernel, shots), out_shape=jax.Sha...]
  transfers between devices with their start and end apart: 1 -> 0, of which waited for: 1 -> 0; matrix products, arithmetic and copies ran while one was open for 0% -> 0% of each run, Pallas kernels for 0% -> 0%
where the time goes in v3:
time: 44.3 us; the launch traced here: 44.1 us
  blocking collectives  35.5 us (80%)
  Pallas kernels  5.89 us (13%)
  local copies, waits for them, and re-layouts  1.45 us (3%)
  other arithmetic  1.14 us (3%)
    all_to_all x1, blocking collectives, gathers_of_all_samples(): lax.all_to_all(restored, ('shot', 'tm'), split_axis=0, concat_axis=0, til...  18.1 us
    all_to_all x1, blocking collectives, gathers_of_all_samples(): lax.all_to_all(sent, ('shot', 'tm'), split_axis=0, concat_axis=0, tiled=T...  17.5 us
    pallas_call x1, Pallas kernels, gathers_of_all_samples(): pl.pallas_call(functools.partial(gather_kernel, shots), out_shape=jax.Sha...  5.89 us
    unnamed x21, local copies, waits for them, and re-layouts  1.45 us
    convert_element_type x1, other arithmetic, gathers_of_all_samples(): lax.optimization_barrier(sent.reshape(count, each, rows, BLK))  1.14 us

profile of v3, /device:TPU:1, one launch (start us, length us, event | category | flops | bytes accessed | tf_op | source)
XLA Modules:
  0.0 44.1 jit_solution(10568824729037001444)
XLA Ops:
  0.0 0.0 copy-start.5
  0.0 0.0 copy-start.6
  0.0 0.0 copy-start.7
  0.0 0.0 copy-start.8
  0.0 0.0 copy-start.9
  0.0 1.1 %convert_element_type.3 = bf16[32,2,16,128]{3,2,1,0:T(8,128)(2,1)S(1)} convert(f32[32,2,16,128]{3,2,1,0:T(8,128)} %bitcast.13) | non-fusion elementwise | flops 131072 | bytes 786432 | tf_op jit(solution)/shard_map/convert_element_type | solution.py:289
  1.2 0.0 copy-start.1
  1.2 0.0 copy-start.2
  1.2 0.0 copy-start.3
  1.2 0.0 copy-start.4
  1.2 17.5 %all_to_all.10.received = bf16[32,2,16,128]{3,2,1,0:T(8,128)(2,1)S(1)} all-to-all(bf16[32,2,16,128]{3,2,1,0:T(8,128)(2,1)S(1)} %convert_element_type.3), channel_id=1, replica_groups=mesh['shot'=16,'tm'=2] {'shot','tm'}, dimensions={0} | all-to-all | bytes 524288 | tf_op jit(solution)/shard_map/all_to_all | solution.py:290
  18.7 0.0 copy-start
  18.7 0.0 copy-done.5
  18.7 0.0 copy-done.6
  18.7 0.0 copy-done.7
  18.7 0.0 copy-done.8
  18.7 0.0 copy-done.9
  18.7 0.0 copy-done.1
  18.7 0.0 copy-done.2
  18.7 0.0 copy-done.3
  18.7 0.0 copy-done.4
  18.8 0.6 %copy-done = s32[32,2]{0,1:T(2,128)S(1)} copy-done((s32[32,2]{0,1:T(2,128)S(1)}, s32[32,2]{0,1:T(2,128)}, u32[]{:S(2)}) %copy-start) | copy-done | bytes 280
  19.4 5.9 %shard_map.109 = bf16[32,2,32,128]{3,2,1,0:T(8,128)(2,1)S(1)} custom-call(s32[2,32]{1,0:T(2,128)S(1)} %bitcast.11, f32[2,64]{1,0:T(2,128)S(1)} %copy-done.1, bf16[32,2,16,128]{3,2,1,0:T(8,128)(2,1)S(1)} %all_to_all.10.received, bf16[256,256]{1,0:T(8,128)(2,1)S(1)} %copy-done.9, bf16[256,256]{1,0:T(8,128)(2,1)S(1)} %copy-done.8, ...), custom_call_target="tpu_custom_call" | custom-call | flops 2415919104 | bytes 2097152 | tf_op jit(solution)/shard_map/pallas_call | solution.py:295
  25.3 18.1 %all_to_all.11 = bf16[32,2,32,128]{3,2,1,0:T(8,128)(2,1)S(1)} all-to-all(bf16[32,2,32,128]{3,2,1,0:T(8,128)(2,1)S(1)} %shard_map.109), channel_id=1, replica_groups=mesh['shot'=16,'tm'=2] {'shot','tm'}, dimensions={0} | all-to-all | bytes 1048576 | tf_op jit(solution)/shard_map/all_to_all | solution.py:315
  43.3 0.8 %copy.15 = bf16[64,4,1024]{2,1,0:T(4,128)(2,1)} copy(bf16[64,4,1024]{2,1,0:T(4,128)(2,1)S(1)} %bitcast.12) | data formatting | bytes 1048576
Async XLA Ops:
  0.0 18.7 %copy-start.5 = (bf16[256,256]{1,0:T(8,128)(2,1)S(1)}, bf16[256,256]{1,0:T(8,128)(2,1)}, u32[]{:S(2)}) copy-start(bf16[256,256]{1,0:T(8,128)(2,1)} %constant.20.clone.backward) | copy-start | bytes 393220
  0.0 18.7 %copy-start.6 = (bf16[256,256]{1,0:T(8,128)(2,1)S(1)}, bf16[256,256]{1,0:T(8,128)(2,1)}, u32[]{:S(2)}) copy-start(bf16[256,256]{1,0:T(8,128)(2,1)} %constant.19.clone.onward) | copy-start | bytes 393220
  0.0 18.7 %copy-start.7 = (bf16[256,256]{1,0:T(8,128)(2,1)S(1)}, bf16[256,256]{1,0:T(8,128)(2,1)}, u32[]{:S(2)}) copy-start(bf16[256,256]{1,0:T(8,128)(2,1)} %constant.18.clone.inverse_low) | copy-start | bytes 393220
  0.0 18.7 %copy-start.8 = (bf16[256,256]{1,0:T(8,128)(2,1)S(1)}, bf16[256,256]{1,0:T(8,128)(2,1)}, u32[]{:S(2)}) copy-start(bf16[256,256]{1,0:T(8,128)(2,1)} %constant.17.clone.inverse_high) | copy-start | bytes 393220
  0.0 18.7 %copy-start.9 = (bf16[256,256]{1,0:T(8,128)(2,1)S(1)}, bf16[256,256]{1,0:T(8,128)(2,1)}, u32[]{:S(2)}) copy-start(bf16[256,256]{1,0:T(8,128)(2,1)} %constant.16.clone.forward) | copy-start | bytes 393220
  1.2 17.5 %copy-start.1 = (f32[2,64]{1,0:T(2,128)S(1)}, f32[2,64]{1,0:T(2,128)}, u32[]{:S(2)}) copy-start(f32[2,64]{1,0:T(2,128)} %limits.1) | copy-start | bytes 1540
  1.2 17.5 %copy-start.2 = (bf16[256,256]{1,0:T(8,128)(2,1)S(1)}, bf16[256,256]{1,0:T(8,128)(2,1)}, u32[]{:S(2)}) copy-start(bf16[256,256]{1,0:T(8,128)(2,1)} %constant.23.clone.order_sources) | copy-start | bytes 393220
  1.2 17.5 %copy-start.3 = (bf16[256,256]{1,0:T(8,128)(2,1)S(1)}, bf16[256,256]{1,0:T(8,128)(2,1)}, u32[]{:S(2)}) copy-start(bf16[256,256]{1,0:T(8,128)(2,1)} %constant.22.clone.order_windows) | copy-start | bytes 393220
  1.2 17.5 %copy-start.4 = (bf16[256,256]{1,0:T(8,128)(2,1)S(1)}, bf16[256,256]{1,0:T(8,128)(2,1)}, u32[]{:S(2)}) copy-start(bf16[256,256]{1,0:T(8,128)(2,1)} %constant.21.clone.order_arrived) | copy-start | bytes 393220
  18.7 0.7 %copy-start = (s32[32,2]{0,1:T(2,128)S(1)}, s32[32,2]{0,1:T(2,128)}, u32[]{:S(2)}) copy-start(s32[32,2]{0,1:T(2,128)} %param.12) | copy-start | bytes 772

commit v4 on v3

--- a/solution.py
+++ b/solution.py
@@ -24,10 +24,12 @@
 TILE = 256
 
 
-def split_table(table):
-    high = table.astype(ml_dtypes.bfloat16)
-    low = (table - high.astype(np.float64)).astype(ml_dtypes.bfloat16)
-    return high, low
+def bfloat_scale(table):
+    values = np.unique(np.abs(table).round(12))
+    factors = 1.0 + np.arange(4096) / 4096.0
+    scaled = factors[:, None] * values
+    lost = scaled.astype(ml_dtypes.bfloat16).astype(np.float64) - scaled
+    return factors[np.argmin(np.sum((lost / factors[:, None]) ** 2, axis=1))]
 
 
 def half_spectrum_tables():
@@ -44,11 +46,16 @@
     turn = (source[:, None] * source[None, :] % SRC) * (2.0 * math.pi / SRC)
     cosine, sine = np.cos(turn) / math.sqrt(SRC), np.sin(turn) / math.sqrt(SRC)
     onward = np.block([[cosine, sine], [-sine, cosine]])
-    pair = []
-    for table in (onward / math.sqrt(WIN), onward.T):
-        high, low = split_table(table)
-        pair.append(np.block([[high, high], [low, low]]))
-    return (forward, *split_table(inverse), *pair)
+    source_scale, time_scale = bfloat_scale(onward), bfloat_scale(inverse)
+    onward = onward * source_scale
+    tables = (
+        forward,
+        inverse * time_scale,
+        np.concatenate([onward, onward], axis=1) / math.sqrt(WIN),
+        np.concatenate([onward.T, onward.T], axis=1),
+    )
+    tables = tuple(table.astype(ml_dtypes.bfloat16) for table in tables)
+    return tables, source_scale, 1.0 / (source_scale * source_scale * time_scale)
 
 
 def rearranging(shape, axes):
@@ -70,35 +77,40 @@
     return high, (value - high.astype(jnp.float32)).astype(jnp.bfloat16)
 
 
-def bfloat(value):
-    return value.astype(jnp.bfloat16).astype(jnp.float32)
-
-
 def product(left, right):
     return jnp.dot(left, right, preferred_element_type=jnp.float32)
 
 
 def gather_kernel(
     shots,
-    delays,
-    limits,
+    limit_scale,
+    kept_scale,
+    delays_far,
+    limits_far,
     received,
     forward,
-    inverse_high,
-    inverse_low,
+    inverse,
     onward,
     backward,
     order_arrived,
     order_windows,
     order_sources,
     out,
+    delays,
+    limits,
     records,
     field,
     mixed,
-    back_high,
-    back_low,
+    back,
     estimates,
+    sems,
 ):
+    copies = [
+        pltpu.make_async_copy(delays_far, delays, sems.at[0]),
+        pltpu.make_async_copy(limits_far, limits, sems.at[1]),
+    ]
+    for copy in copies:
+        copy.start()
     count, receivers, rows, _ = received.shape
     blocks_of_time = count // shots
     experiments, sources = delays.shape[1], SRC
@@ -115,6 +127,9 @@
         senders = slice(chunk * TILE // rows, (chunk + 1) * TILE // rows)
         arrived = [received[senders, r].reshape(TILE, BLK) for r in range(receivers)]
         records[chunk] = product(order_arrived[...], jnp.concatenate(arrived, axis=1))
+
+    for copy in copies:
+        copy.wait()
 
     def advanced(even, odd, delay):
         by = (BLK - delay) & (BLK - 1)
@@ -156,8 +171,8 @@
                     for k in range(SRC_EXP)
                 ]
                 late = [delayed(*estimate[k], lags[k]) for k in range(SRC_EXP)]
-                even = bfloat(even - sum(x[0] for x in late))
-                odd = bfloat(odd - sum(x[1] for x in late))
+                even = even - sum(x[0] for x in late)
+                odd = odd - sum(x[1] for x in late)
             for k in range(SRC_EXP):
                 values = [RELAX * x for x in advanced(even, odd, lags[k])]
                 if sweep > 0:
@@ -166,9 +181,9 @@
         return jnp.concatenate(updated, axis=0).astype(jnp.bfloat16)
 
     def update_and_forward_in_time(sweep):
-        for chunk in range(sources // some):
-            nyquist = jnp.zeros((some, HALF), jnp.float32)
-            for r in range(receivers):
+        nyquists = [jnp.zeros((some, HALF), jnp.float32) for _ in range(sources // some)]
+        for r in range(receivers):
+            for chunk in range(sources // some):
                 signal = product(order_windows[...], update(sweep, r, chunk))
                 spectra = product(signal.astype(jnp.bfloat16), forward[...])
                 for w in range(windows):
@@ -176,9 +191,10 @@
                     spectrum = spectra[w * some : (w + 1) * some]
                     real, imag = spectrum[:, :HALF], spectrum[:, HALF:]
                     moved = pltpu.roll(imag, group, 1) if group else imag
-                    nyquist = jnp.where(lane_of_some == group, moved, nyquist)
+                    nyquists[chunk] = jnp.where(lane_of_some == group, moved, nyquists[chunk])
                     imag = jnp.where(lane_of_some == 0, 0.0, imag)
                     put(field, columns(group), real, imag, chunk * some)
+        for chunk, nyquist in enumerate(nyquists):
             put(field, columns(groups), nyquist, jnp.zeros_like(nyquist), chunk * some)
 
     def put(ref, where, real, imag, first=0):
@@ -194,12 +210,11 @@
             yield columns(group, 2)
 
     def mixing(table, ref, where):
-        both = product(table[...], ref[:, where])
-        total = both[: 2 * sources] + both[2 * sources :]
+        total = product(table[...], ref[:, where])
         return total[:sources], total[sources:]
 
     def shrink(sweep):
-        limit = limits[sweep : sweep + 1, :]
+        limit = limits[sweep : sweep + 1, :] * (limit_scale * kept_scale)
         p = lax.broadcasted_iota(jnp.int32, (sources, sources), 0)
         q = lax.broadcasted_iota(jnp.int32, (sources, sources), 1)
         bound = jnp.sum(jnp.where(p == q, limit, 0.0), axis=1, keepdims=True)
@@ -208,8 +223,8 @@
         for where in chunks():
             real, imag = mixing(onward, field, where)
             inverse_size = lax.rsqrt(real * real + imag * imag)
-            factor = jnp.maximum(1.0 - bound * inverse_size, 0.0) + jnp.maximum(
-                1.0 - bound_mirrored * inverse_size, 0.0
+            factor = jnp.maximum(kept_scale - bound * inverse_size, 0.0) + jnp.maximum(
+                kept_scale - bound_mirrored * inverse_size, 0.0
             )
             put(mixed, where, real * factor, imag * factor)
 
@@ -227,18 +242,8 @@
                 own_imag = jnp.where(lane_of_group == 0, moved, own_imag)
                 rows_of_group = slice(group * sources, (group + 1) * sources)
                 for half, value in enumerate((own_real, own_imag)):
-                    high, low = halves(value)
-                    back_high[rows_of_group, columns(half)] = high
-                    back_low[rows_of_group, columns(half)] = low
+                    back[rows_of_group, columns(half)] = value.astype(jnp.bfloat16)
                 group += 1
-
-    def back_in_time(rows_of_span):
-        high = back_high[rows_of_span, :]
-        return (
-            product(high, inverse_high[...])
-            + product(back_low[rows_of_span, :], inverse_high[...])
-            + product(high, inverse_low[...])
-        )
 
     def swapped(value):
         return pltpu.roll(value, SUB // 2, 1)
@@ -267,7 +272,7 @@
         back_in_source()
         for start in range(0, groups, SPAN):
             rows_of_span = slice(start * sources, (start + SPAN) * sources)
-            restored = back_in_time(rows_of_span)
+            restored = product(back[rows_of_span, :], inverse[...])
             if sweep < ITERS - 1:
                 estimates[rows_of_span, :] = restored.astype(jnp.bfloat16)
                 continue
@@ -288,26 +293,28 @@
     sent = blended.reshape(receivers, own, blocks, BLK).transpose(0, 2, 1, 3)
     sent = lax.optimization_barrier(sent.reshape(count, each, rows, BLK)).astype(jnp.bfloat16)
     received = lax.all_to_all(sent, ("shot", "tm"), split_axis=0, concat_axis=0, tiled=True)
-    tables = half_spectrum_tables() + order_tables(windows, own)
-    tables = [jnp.asarray(table) for table in tables]
-    vmem = pl.BlockSpec(memory_space=pltpu.VMEM)
+    tables, limit_scale, kept_scale = half_spectrum_tables()
+    tables = [jnp.asarray(table) for table in tables + order_tables(windows, own)]
+    vmem, far = pl.BlockSpec(memory_space=pltpu.VMEM), pl.BlockSpec(memory_space=pltpu.HBM)
     held = SRC // shots
     restored = pl.pallas_call(
-        functools.partial(gather_kernel, shots),
+        functools.partial(gather_kernel, shots, float(limit_scale), float(kept_scale)),
         out_shape=jax.ShapeDtypeStruct((count, each, blocks * held, BLK), jnp.bfloat16),
-        in_specs=[pl.BlockSpec(memory_space=pltpu.SMEM)] + [vmem] * (2 + len(tables)),
+        in_specs=[far] * 2 + [vmem] * (1 + len(tables)),
         out_specs=vmem,
         scratch_shapes=[
+            pltpu.SMEM(delays.T.shape, jnp.int32),
+            pltpu.VMEM(thresholds.shape, jnp.float32),
             pltpu.VMEM((SRC * windows // TILE, TILE, each * BLK), jnp.float32),
             pltpu.VMEM((4 * SRC, (groups + 1) * HALF), jnp.bfloat16),
             pltpu.VMEM((4 * SRC, (groups + 1) * HALF), jnp.bfloat16),
             pltpu.VMEM((groups * SRC, WIN), jnp.bfloat16),
             pltpu.VMEM((groups * SRC, WIN), jnp.bfloat16),
-            pltpu.VMEM((groups * SRC, WIN), jnp.bfloat16),
+            pltpu.SemaphoreType.DMA((2,)),
         ],
         compiler_params=pltpu.CompilerParams(vmem_limit_bytes=40 * 1024 * 1024),
         cost_estimate=pl.CostEstimate(
-            flops=2 * ITERS * groups * SRC * WIN * WIN * 9,
+            flops=2 * ITERS * groups * SRC * WIN * WIN * 5,
             bytes_accessed=2 * 1024 * 1024,
             transcendentals=ITERS * groups * SRC * HALF,
         ),

time: 44.3 us -> 43.3 us (0.977)
  Pallas kernels: 5.89 us -> 4.85 us
    pallas_call x1, Pallas kernels: 5.89 us -> 4.85 us  [gathers_of_all_samples(): pl.pallas_call(functools.partial(gather_kernel, shots, float(limit_scale)...]
    unnamed x21 -> x19, local copies, waits for them, and re-layouts: 1.45 us -> 1.46 us
where the time goes in v4:
time: 43.3 us; the launch traced here: 43.1 us
  blocking collectives  35.5 us (82%)
  Pallas kernels  4.85 us (11%)
  local copies, waits for them, and re-layouts  1.46 us (3%)
  other arithmetic  1.13 us (3%)
    all_to_all x1, blocking collectives, gathers_of_all_samples(): lax.all_to_all(restored, ('shot', 'tm'), split_axis=0, concat_axis=0, til...  18.1 us
    all_to_all x1, blocking collectives, gathers_of_all_samples(): lax.all_to_all(sent, ('shot', 'tm'), split_axis=0, concat_axis=0, tiled=T...  17.5 us
    pallas_call x1, Pallas kernels, gathers_of_all_samples(): pl.pallas_call(functools.partial(gather_kernel, shots, float(limit_scale)...  4.85 us
    unnamed x19, local copies, waits for them, and re-layouts  1.46 us
    convert_element_type x1, other arithmetic, gathers_of_all_samples(): lax.optimization_barrier(sent.reshape(count, each, rows, BLK))  1.13 us

profile of v4, /device:TPU:1, one launch (start us, length us, event | category | flops | bytes accessed | tf_op | source)
XLA Modules:
  0.0 43.1 jit_solution(8047970049122167758)
XLA Ops:
  0.0 0.0 copy-start.5
  0.0 0.0 copy-start.6
  0.0 0.0 copy-start.8
  0.0 1.1 %convert_element_type.3 = bf16[32,2,16,128]{3,2,1,0:T(8,128)(2,1)S(1)} convert(f32[32,2,16,128]{3,2,1,0:T(8,128)} %bitcast.13) | non-fusion elementwise | flops 131072 | bytes 786432 | tf_op jit(solution)/shard_map/convert_element_type | solution.py:294
  1.1 0.0 copy-start.1
  1.2 0.0 copy-start.2
  1.2 0.0 copy-start.3
  1.2 0.0 copy-start.4
  1.2 0.0 copy-start.7
  1.2 17.5 %all_to_all.10.received = bf16[32,2,16,128]{3,2,1,0:T(8,128)(2,1)S(1)} all-to-all(bf16[32,2,16,128]{3,2,1,0:T(8,128)(2,1)S(1)} %convert_element_type.3), channel_id=1, replica_groups=mesh['shot'=16,'tm'=2] {'shot','tm'}, dimensions={0} | all-to-all | bytes 524288 | tf_op jit(solution)/shard_map/all_to_all | solution.py:295
  18.7 0.0 copy-start
  18.7 0.0 copy-done.5
  18.7 0.0 copy-done.6
  18.7 0.0 copy-done.8
  18.7 0.0 copy-done.1
  18.7 0.0 copy-done.2
  18.7 0.0 copy-done.3
  18.7 0.0 copy-done.4
  18.7 0.0 copy-done.7
  18.7 0.6 %copy-done = s32[32,2]{0,1:T(2,128)S(1)} copy-done((s32[32,2]{0,1:T(2,128)S(1)}, s32[32,2]{0,1:T(2,128)}, u32[]{:S(2)}) %copy-start) | copy-done | bytes 280
  19.3 4.9 %shard_map.100 = bf16[32,2,32,128]{3,2,1,0:T(8,128)(2,1)S(1)} custom-call(s32[2,32]{1,0:T(2,128)S(1)} %bitcast.11, f32[2,64]{1,0:T(2,128)S(1)} %copy-done.1, bf16[32,2,16,128]{3,2,1,0:T(8,128)(2,1)S(1)} %all_to_all.10.received, bf16[256,256]{1,0:T(8,128)(2,1)S(1)} %copy-done.6, bf16[256,256]{1,0:T(8,128)(2,1)S(1)} %copy-done.5, ...), custom_call_target="tpu_custom_call" | custom-call | flops 1342177280 | bytes 2097152 | tf_op jit(solution)/shard_map/pallas_call | solution.py:300
  24.2 18.1 %all_to_all.11 = bf16[32,2,32,128]{3,2,1,0:T(8,128)(2,1)S(1)} all-to-all(bf16[32,2,32,128]{3,2,1,0:T(8,128)(2,1)S(1)} %shard_map.100), channel_id=1, replica_groups=mesh['shot'=16,'tm'=2] {'shot','tm'}, dimensions={0} | all-to-all | bytes 1048576 | tf_op jit(solution)/shard_map/all_to_all | solution.py:322
  42.3 0.8 %copy.14 = bf16[64,4,1024]{2,1,0:T(4,128)(2,1)} copy(bf16[64,4,1024]{2,1,0:T(4,128)(2,1)S(1)} %bitcast.12) | data formatting | bytes 1048576
Async XLA Ops:
  0.0 18.7 %copy-start.5 = (bf16[256,256]{1,0:T(8,128)(2,1)S(1)}, bf16[256,256]{1,0:T(8,128)(2,1)}, u32[]{:S(2)}) copy-start(bf16[256,256]{1,0:T(8,128)(2,1)} %constant.15.clone.inverse) | copy-start | bytes 393220
  0.0 18.7 %copy-start.6 = (bf16[256,256]{1,0:T(8,128)(2,1)S(1)}, bf16[256,256]{1,0:T(8,128)(2,1)}, u32[]{:S(2)}) copy-start(bf16[256,256]{1,0:T(8,128)(2,1)} %constant.14.clone.forward) | copy-start | bytes 393220
  0.0 18.7 %copy-start.8 = (bf16[128,256]{1,0:T(8,128)(2,1)S(1)}, bf16[128,256]{1,0:T(8,128)(2,1)}, u32[]{:S(2)}) copy-start(bf16[128,256]{1,0:T(8,128)(2,1)} %constant.16.clone.onward) | copy-start | bytes 196612
  1.1 17.5 %copy-start.1 = (f32[2,64]{1,0:T(2,128)S(1)}, f32[2,64]{1,0:T(2,128)}, u32[]{:S(2)}) copy-start(f32[2,64]{1,0:T(2,128)} %limits_far.1) | copy-start | bytes 1540
  1.2 17.5 %copy-start.2 = (bf16[256,256]{1,0:T(8,128)(2,1)S(1)}, bf16[256,256]{1,0:T(8,128)(2,1)}, u32[]{:S(2)}) copy-start(bf16[256,256]{1,0:T(8,128)(2,1)} %constant.20.clone.order_sources) | copy-start | bytes 393220
  1.2 17.5 %copy-start.3 = (bf16[256,256]{1,0:T(8,128)(2,1)S(1)}, bf16[256,256]{1,0:T(8,128)(2,1)}, u32[]{:S(2)}) copy-start(bf16[256,256]{1,0:T(8,128)(2,1)} %constant.19.clone.order_windows) | copy-start | bytes 393220
  1.2 17.5 %copy-start.4 = (bf16[256,256]{1,0:T(8,128)(2,1)S(1)}, bf16[256,256]{1,0:T(8,128)(2,1)}, u32[]{:S(2)}) copy-start(bf16[256,256]{1,0:T(8,128)(2,1)} %constant.18.clone.order_arrived) | copy-start | bytes 393220
  1.2 17.5 %copy-start.7 = (bf16[128,256]{1,0:T(8,128)(2,1)S(1)}, bf16[128,256]{1,0:T(8,128)(2,1)}, u32[]{:S(2)}) copy-start(bf16[128,256]{1,0:T(8,128)(2,1)} %constant.17.clone.backward) | copy-start | bytes 196612
  18.7 0.7 %copy-start = (s32[32,2]{0,1:T(2,128)S(1)}, s32[32,2]{0,1:T(2,128)}, u32[]{:S(2)}) copy-start(s32[32,2]{0,1:T(2,128)} %param.11) | copy-start | bytes 772

commit v5 on v4

--- a/solution.py
+++ b/solution.py
@@ -86,31 +86,27 @@
     limit_scale,
     kept_scale,
     delays_far,
-    limits_far,
+    limits,
     received,
-    forward,
-    inverse,
-    onward,
-    backward,
-    order_arrived,
-    order_windows,
-    order_sources,
+    tables,
     out,
     delays,
-    limits,
     records,
     field,
     mixed,
     back,
+    firsts,
     estimates,
-    sems,
+    sem,
 ):
-    copies = [
-        pltpu.make_async_copy(delays_far, delays, sems.at[0]),
-        pltpu.make_async_copy(limits_far, limits, sems.at[1]),
-    ]
-    for copy in copies:
-        copy.start()
+    copy = pltpu.make_async_copy(delays_far, delays, sem)
+    copy.start()
+    forward, inverse, order_arrived, order_windows, order_sources = (
+        tables.at[pl.ds(at * TILE, TILE)] for at in range(5)
+    )
+    onward, backward = (
+        tables.at[pl.ds(5 * TILE + at * 2 * SRC, 2 * SRC)] for at in range(2)
+    )
     count, receivers, rows, _ = received.shape
     blocks_of_time = count // shots
     experiments, sources = delays.shape[1], SRC
@@ -128,8 +124,7 @@
         arrived = [received[senders, r].reshape(TILE, BLK) for r in range(receivers)]
         records[chunk] = product(order_arrived[...], jnp.concatenate(arrived, axis=1))
 
-    for copy in copies:
-        copy.wait()
+    copy.wait()
 
     def advanced(even, odd, delay):
         by = (BLK - delay) & (BLK - 1)
@@ -138,53 +133,70 @@
         same = lane < BLK - delay
         return jnp.where(same, even, odd), jnp.where(same, odd, after)
 
-    def delayed(even, odd, delay):
-        even, odd = pltpu.roll(even, delay, 1), pltpu.roll(odd, delay, 1)
-        before = jnp.where(row > 0, pltpu.roll(odd, 1, 0), 0.0)
-        same = lane >= delay
-        return jnp.where(same, even, before), jnp.where(same, odd, even)
+    def moved_by(even, odd, ahead_by):
+        ahead = ahead_by >= 0
+        by = (BLK - ahead_by) & (BLK - 1)
+        even, odd = pltpu.roll(even, by, 1), pltpu.roll(odd, by, 1)
+        other = pltpu.roll(jnp.where(ahead, even, odd), jnp.where(ahead, windows - 1, 1), 0)
+        other = jnp.where(row != jnp.where(ahead, windows - 1, 0), other, 0.0)
+        same = ((lane + ahead_by) & -BLK) == 0
+        return (
+            jnp.where(same, even, jnp.where(ahead, odd, other)),
+            jnp.where(same, odd, jnp.where(ahead, other, even)),
+        )
 
     def columns(group, many=1):
         return slice(group * HALF, (group + many) * HALF)
 
-    def update(sweep, r, chunk):
-        if sweep > 0:
-            before = [
-                estimates[pl.ds((r * windows + w) * sources + chunk * some, some), :]
-                for w in range(windows)
-            ]
-            before = product(order_sources[...], jnp.concatenate(before, axis=0))
+    def first_update(r, chunk):
         updated = []
         for at in range(0, some, SRC_EXP):
-            experiment = (chunk * some + at) // SRC_EXP
-            lags = [delays[k, experiment] for k in range(SRC_EXP)]
             even, odd = (
                 records[chunk, pl.ds((at + half) * windows, windows), columns(r)]
                 for half in range(2)
             )
-            if sweep > 0:
-                estimate = [
-                    tuple(
-                        before[(at + k) * windows : (at + k + 1) * windows, columns(half)]
-                        for half in range(2)
-                    )
-                    for k in range(SRC_EXP)
-                ]
-                late = [delayed(*estimate[k], lags[k]) for k in range(SRC_EXP)]
-                even = even - sum(x[0] for x in late)
-                odd = odd - sum(x[1] for x in late)
             for k in range(SRC_EXP):
-                values = [RELAX * x for x in advanced(even, odd, lags[k])]
-                if sweep > 0:
-                    values = [a + b for a, b in zip(estimate[k], values)]
-                updated.append(jnp.concatenate(values, axis=1))
+                early = advanced(even, odd, delays[k, (chunk * some + at) // SRC_EXP])
+                updated.append(jnp.concatenate([RELAX * x for x in early], axis=1))
+        updated = jnp.concatenate(updated, axis=0).astype(jnp.bfloat16)
+        firsts[pl.ds((r * sources + chunk * some) * windows, TILE), :] = updated
+        return updated
+
+    def later_update(r, chunk):
+        before = [
+            estimates[pl.ds((r * windows + w) * sources + chunk * some, some), :]
+            for w in range(windows)
+        ]
+        before = product(order_sources[...], jnp.concatenate(before, axis=0))
+        first = (r * sources + chunk * some) * windows
+        updated = []
+        for at in range(0, some, SRC_EXP):
+            lags = [delays[k, (chunk * some + at) // SRC_EXP] for k in range(SRC_EXP)]
+            spread = firsts[pl.ds(first + at * windows, SRC_EXP * windows), :]
+            spread = spread.astype(jnp.float32)
+            estimate = [
+                tuple(
+                    before[(at + k) * windows : (at + k + 1) * windows, columns(half)]
+                    for half in range(2)
+                )
+                for k in range(SRC_EXP)
+            ]
+            for k in range(SRC_EXP):
+                even, odd = estimate[k]
+                other = moved_by(*estimate[1 - k], lags[k] - lags[1 - k])
+                stays = (row < windows - 1) | (lane < BLK - lags[k])
+                even = RELAX * (even - other[0])
+                odd = jnp.where(stays, RELAX * (odd - other[1]), odd)
+                step = spread[k * windows : (k + 1) * windows]
+                updated.append(jnp.concatenate([even, odd], axis=1) + step)
         return jnp.concatenate(updated, axis=0).astype(jnp.bfloat16)
 
     def update_and_forward_in_time(sweep):
         nyquists = [jnp.zeros((some, HALF), jnp.float32) for _ in range(sources // some)]
         for r in range(receivers):
             for chunk in range(sources // some):
-                signal = product(order_windows[...], update(sweep, r, chunk))
+                update = later_update if sweep else first_update
+                signal = product(order_windows[...], update(r, chunk))
                 spectra = product(signal.astype(jnp.bfloat16), forward[...])
                 for w in range(windows):
                     group = r * windows + w
@@ -281,6 +293,12 @@
                 deliver((start + group) // windows, (start + group) % windows, pair)
 
 
+def cast_kernel(blended, delays, limits, sent, delays_near, limits_near):
+    sent[...] = blended[...].astype(jnp.bfloat16)
+    delays_near[...] = delays[...]
+    limits_near[...] = limits[...]
+
+
 def gathers_of_all_samples(shots, blended, delays, thresholds):
     receivers, own, samples = blended.shape
     blocks_of_time = lax.axis_size("tm")
@@ -291,26 +309,37 @@
     groups = each * windows
     rows = blocks * own
     sent = blended.reshape(receivers, own, blocks, BLK).transpose(0, 2, 1, 3)
-    sent = lax.optimization_barrier(sent.reshape(count, each, rows, BLK)).astype(jnp.bfloat16)
+    sent = sent.reshape(count, each, rows, BLK)
+    vmem = pl.BlockSpec(memory_space=pltpu.VMEM)
+    sent, delays, thresholds = pl.pallas_call(
+        cast_kernel,
+        out_shape=(
+            jax.ShapeDtypeStruct(sent.shape, jnp.bfloat16),
+            jax.ShapeDtypeStruct(delays.T.shape, delays.dtype),
+            jax.ShapeDtypeStruct(thresholds.shape, thresholds.dtype),
+        ),
+        in_specs=[vmem] * 3,
+        out_specs=[vmem] * 3,
+        compiler_params=pltpu.CompilerParams(vmem_limit_bytes=8 * 1024 * 1024),
+    )(sent, delays.T, thresholds)
     received = lax.all_to_all(sent, ("shot", "tm"), split_axis=0, concat_axis=0, tiled=True)
     tables, limit_scale, kept_scale = half_spectrum_tables()
-    tables = [jnp.asarray(table) for table in tables + order_tables(windows, own)]
-    vmem, far = pl.BlockSpec(memory_space=pltpu.VMEM), pl.BlockSpec(memory_space=pltpu.HBM)
+    tables = np.concatenate(tables[:2] + order_tables(windows, own) + tables[2:], axis=0)
     held = SRC // shots
     restored = pl.pallas_call(
         functools.partial(gather_kernel, shots, float(limit_scale), float(kept_scale)),
         out_shape=jax.ShapeDtypeStruct((count, each, blocks * held, BLK), jnp.bfloat16),
-        in_specs=[far] * 2 + [vmem] * (1 + len(tables)),
+        in_specs=[pl.BlockSpec(memory_space=pl.ANY)] + [vmem] * 3,
         out_specs=vmem,
         scratch_shapes=[
-            pltpu.SMEM(delays.T.shape, jnp.int32),
-            pltpu.VMEM(thresholds.shape, jnp.float32),
+            pltpu.SMEM(delays.shape, jnp.int32),
             pltpu.VMEM((SRC * windows // TILE, TILE, each * BLK), jnp.float32),
             pltpu.VMEM((4 * SRC, (groups + 1) * HALF), jnp.bfloat16),
             pltpu.VMEM((4 * SRC, (groups + 1) * HALF), jnp.bfloat16),
             pltpu.VMEM((groups * SRC, WIN), jnp.bfloat16),
             pltpu.VMEM((groups * SRC, WIN), jnp.bfloat16),
-            pltpu.SemaphoreType.DMA((2,)),
+            pltpu.VMEM((groups * SRC, WIN), jnp.bfloat16),
+            pltpu.SemaphoreType.DMA(()),
         ],
         compiler_params=pltpu.CompilerParams(vmem_limit_bytes=40 * 1024 * 1024),
         cost_estimate=pl.CostEstimate(
@@ -318,7 +347,7 @@
             bytes_accessed=2 * 1024 * 1024,
             transcendentals=ITERS * groups * SRC * HALF,
         ),
-    )(delays.T, thresholds, received, *tables)
+    )(delays, thresholds, received, jnp.asarray(tables))
     final = lax.all_to_all(restored, ("shot", "tm"), split_axis=0, concat_axis=0, tiled=True)
     final = final.reshape(receivers, blocks, held, BLK).transpose(0, 2, 1, 3)
     return final.reshape(receivers, held, samples)

time: 43.3 us -> 43.3 us (level)
  other arithmetic: 1.13 us -> 0 us
  local copies, waits for them, and re-layouts: 1.46 us -> 2.53 us
    convert_element_type x1 -> x0, other arithmetic: 1.13 us -> none  [gathers_of_all_samples(): lax.optimization_barrier(sent.reshape(count, each, rows, BLK))]
    unnamed x19 -> x9, local copies, waits for them, and re-layouts: 1.46 us -> 2.53 us
where the time goes in v5:
time: 43.3 us; the launch traced here: 43.1 us
  blocking collectives  35.5 us (82%)
  Pallas kernels  5 us (12%)
  local copies, waits for them, and re-layouts  2.53 us (6%)
    all_to_all x1, blocking collectives, gathers_of_all_samples(): lax.all_to_all(restored, ('shot', 'tm'), split_axis=0, concat_axis=0, til...  18.1 us
    all_to_all x1, blocking collectives, gathers_of_all_samples(): lax.all_to_all(sent, ('shot', 'tm'), split_axis=0, concat_axis=0, tiled=T...  17.5 us
    pallas_call x1, Pallas kernels, gathers_of_all_samples(): pl.pallas_call(functools.partial(gather_kernel, shots, float(limit_scale)...  4.98 us
    unnamed x9, local copies, waits for them, and re-layouts  2.53 us

profile of v5, /device:TPU:1, one launch (start us, length us, event | category | flops | bytes accessed | tf_op | source)
XLA Modules:
  0.0 43.1 jit_solution(9128828025115212211)
XLA Ops:
  0.0 0.0 copy-start.2
  0.0 0.0 copy-start.1
  0.0 0.7 %copy-done.2 = f32[2,64]{1,0:T(2,128)S(1)} copy-done((f32[2,64]{1,0:T(2,128)S(1)}, f32[2,64]{1,0:T(2,128)}, u32[]{:S(2)}) %copy-start.2) | copy-done | bytes 536
  0.7 0.0 copy-done.1
  0.7 0.0 copy-start
  0.7 1.0 %copy-done = f32[64,2,1024]{2,1,0:T(2,128)S(1)} copy-done((f32[64,2,1024]{2,1,0:T(2,128)S(1)}, f32[64,2,1024]{2,1,0:T(2,128)}, u32[]{:S(2)}) %copy-start) | copy-done | bytes 524312
  1.7 0.0 copy-start.3
  1.8 17.5 %all_to_all.10.received = bf16[32,2,16,128]{3,2,1,0:T(8,128)(2,1)S(1)} all-to-all(bf16[32,2,16,128]{3,2,1,0:T(8,128)(2,1)S(1)} %get-tuple-element.10), channel_id=1, replica_groups=mesh['shot'=16,'tm'=2] {'shot','tm'}, dimensions={0} | all-to-all | bytes 524288 | tf_op jit(solution)/shard_map/all_to_all | solution.py:325
  19.2 0.0 copy-done.3
  19.2 5.0 %shard_map.47 = bf16[32,2,32,128]{3,2,1,0:T(8,128)(2,1)S(1)} custom-call(s32[2,32]{1,0:T(2,128)S(1)} %get-tuple-element.8.delays_far, f32[2,64]{1,0:T(2,128)S(1)} %get-tuple-element.9.limits, bf16[32,2,16,128]{3,2,1,0:T(8,128)(2,1)S(1)} %all_to_all.10.received, bf16[1536,256]{1,0:T(8,128)(2,1)S(1)} %copy-done.3), custom_call_target="tpu_custom_call" | custom-call | flops 1342177280 | bytes 2097152 | tf_op jit(solution)/shard_map/pallas_call | solution.py:329
  24.2 18.1 %all_to_all.11 = bf16[32,2,32,128]{3,2,1,0:T(8,128)(2,1)S(1)} all-to-all(bf16[32,2,32,128]{3,2,1,0:T(8,128)(2,1)S(1)} %shard_map.47), channel_id=1, replica_groups=mesh['shot'=16,'tm'=2] {'shot','tm'}, dimensions={0} | all-to-all | bytes 1048576 | tf_op jit(solution)/shard_map/all_to_all | solution.py:351
  42.3 0.8 %copy.8 = bf16[64,4,1024]{2,1,0:T(4,128)(2,1)} copy(bf16[64,4,1024]{2,1,0:T(4,128)(2,1)S(1)} %bitcast.13) | data formatting | bytes 1048576
  (1 shorter events, 0.0 us)
Async XLA Ops:
  0.0 0.7 %copy-start.2 = (f32[2,64]{1,0:T(2,128)S(1)}, f32[2,64]{1,0:T(2,128)}, u32[]{:S(2)}) copy-start(f32[2,64]{1,0:T(2,128)} %limits.1) | copy-start | bytes 1540
  0.0 0.7 %copy-start.1 = (s32[32,2]{0,1:T(2,128)S(1)}, s32[32,2]{0,1:T(2,128)}, u32[]{:S(2)}) copy-start(s32[32,2]{0,1:T(2,128)} %param.5) | copy-start | bytes 772
  0.7 1.0 %copy-start = (f32[64,2,1024]{2,1,0:T(2,128)S(1)}, f32[64,2,1024]{2,1,0:T(2,128)}, u32[]{:S(2)}) copy-start(f32[64,2,1024]{2,1,0:T(2,128)} %param.4) | copy-start | bytes 1572868
  1.7 17.5 %copy-start.3 = (bf16[1536,256]{1,0:T(8,128)(2,1)S(1)}, bf16[1536,256]{1,0:T(8,128)(2,1)}, u32[]{:S(2)}) copy-start(bf16[1536,256]{1,0:T(8,128)(2,1)} %constant.2.clone.tables) | copy-start | bytes 2359300

commit v6 on v5

--- a/solution.py
+++ b/solution.py
@@ -81,26 +81,35 @@
     return jnp.dot(left, right, preferred_element_type=jnp.float32)
 
 
+def interleaved(*steps):
+    steps = list(steps)
+    while steps:
+        steps = [step for step in steps if next(step, step) is not step]
+
+
 def gather_kernel(
     shots,
     limit_scale,
     kept_scale,
     delays_far,
-    limits,
+    limits_far,
     received,
     tables,
     out,
     delays,
+    limits,
     records,
     field,
-    mixed,
-    back,
     firsts,
     estimates,
-    sem,
+    sems,
 ):
-    copy = pltpu.make_async_copy(delays_far, delays, sem)
-    copy.start()
+    copies = [
+        pltpu.make_async_copy(delays_far, delays, sems.at[0]),
+        pltpu.make_async_copy(limits_far, limits, sems.at[1]),
+    ]
+    for copy in copies:
+        copy.start()
     forward, inverse, order_arrived, order_windows, order_sources = (
         tables.at[pl.ds(at * TILE, TILE)] for at in range(5)
     )
@@ -124,7 +133,8 @@
         arrived = [received[senders, r].reshape(TILE, BLK) for r in range(receivers)]
         records[chunk] = product(order_arrived[...], jnp.concatenate(arrived, axis=1))
 
-    copy.wait()
+    for copy in copies:
+        copy.wait()
 
     def advanced(even, odd, delay):
         by = (BLK - delay) & (BLK - 1)
@@ -191,71 +201,79 @@
                 updated.append(jnp.concatenate([even, odd], axis=1) + step)
         return jnp.concatenate(updated, axis=0).astype(jnp.bfloat16)
 
-    def update_and_forward_in_time(sweep):
-        nyquists = [jnp.zeros((some, HALF), jnp.float32) for _ in range(sources // some)]
-        for r in range(receivers):
-            for chunk in range(sources // some):
-                update = later_update if sweep else first_update
-                signal = product(order_windows[...], update(r, chunk))
-                spectra = product(signal.astype(jnp.bfloat16), forward[...])
-                for w in range(windows):
-                    group = r * windows + w
-                    spectrum = spectra[w * some : (w + 1) * some]
-                    real, imag = spectrum[:, :HALF], spectrum[:, HALF:]
-                    moved = pltpu.roll(imag, group, 1) if group else imag
-                    nyquists[chunk] = jnp.where(lane_of_some == group, moved, nyquists[chunk])
-                    imag = jnp.where(lane_of_some == 0, 0.0, imag)
-                    put(field, columns(group), real, imag, chunk * some)
-        for chunk, nyquist in enumerate(nyquists):
-            put(field, columns(groups), nyquist, jnp.zeros_like(nyquist), chunk * some)
-
-    def put(ref, where, real, imag, first=0):
+    def parts_of(real, imag):
         real_high, real_low = halves(real)
         imag_high, imag_low = halves(imag)
-        for at, value in enumerate((real_high, imag_high, real_low, imag_low)):
+        return real_high, imag_high, real_low, imag_low
+
+    def put(r, where, real, imag, first):
+        for at, value in enumerate(parts_of(real, imag)):
             start = at * sources + first
-            ref[start : start + value.shape[0], where] = value
-
-    def chunks():
-        yield columns(groups)
-        for group in range(0, groups, 2):
-            yield columns(group, 2)
-
-    def mixing(table, ref, where):
-        total = product(table[...], ref[:, where])
-        return total[:sources], total[sources:]
-
-    def shrink(sweep):
+            field[r, start : start + value.shape[0], where] = value
+
+    def onward_steps(sweep, r):
+        update = later_update if sweep else first_update
+        for chunk in range(sources // some):
+            updated = update(r, chunk)
+            yield
+            signal = product(order_windows[...], updated).astype(jnp.bfloat16)
+            yield
+            spectra = product(signal, forward[...])
+            yield
+            nyquist = jnp.zeros((some, HALF), jnp.float32)
+            for w in range(windows):
+                spectrum = spectra[w * some : (w + 1) * some]
+                real, imag = spectrum[:, :HALF], spectrum[:, HALF:]
+                moved = pltpu.roll(imag, w, 1) if w else imag
+                nyquist = jnp.where(lane_of_some == w, moved, nyquist)
+                imag = jnp.where(lane_of_some == 0, 0.0, imag)
+                put(r, columns(w), real, imag, chunk * some)
+            put(r, columns(windows), nyquist, jnp.zeros_like(nyquist), chunk * some)
+            yield
+
+    def bounds_of(sweep):
         limit = limits[sweep : sweep + 1, :] * (limit_scale * kept_scale)
         p = lax.broadcasted_iota(jnp.int32, (sources, sources), 0)
         q = lax.broadcasted_iota(jnp.int32, (sources, sources), 1)
-        bound = jnp.sum(jnp.where(p == q, limit, 0.0), axis=1, keepdims=True)
         mirrored = (p + q == 0) | (p + q == sources)
-        bound_mirrored = jnp.sum(jnp.where(mirrored, limit, 0.0), axis=1, keepdims=True)
-        for where in chunks():
-            real, imag = mixing(onward, field, where)
-            inverse_size = lax.rsqrt(real * real + imag * imag)
-            factor = jnp.maximum(kept_scale - bound * inverse_size, 0.0) + jnp.maximum(
-                kept_scale - bound_mirrored * inverse_size, 0.0
-            )
-            put(mixed, where, real * factor, imag * factor)
-
-    def back_in_source():
+        return [
+            jnp.sum(jnp.where(at, limit, 0.0), axis=1, keepdims=True) for at in (p == q, mirrored)
+        ]
+
+    def shrunk(bounds, real, imag):
+        inverse_size = lax.rsqrt(real * real + imag * imag)
+        factor = sum(jnp.maximum(kept_scale - bound * inverse_size, 0.0) for bound in bounds)
+        return jnp.concatenate(parts_of(real * factor, imag * factor), axis=0)
+
+    def backward_steps(sweep, r):
         nyquist = None
-        group = 0
-        for where in chunks():
-            real, imag = mixing(backward, mixed, where)
+        for first in (windows, *range(0, windows, 2)):
+            coefficients = product(onward[...], field[r, :, columns(first, min(2, windows + 1 - first))])
+            yield
+            kept = shrunk(bounds[sweep], coefficients[:sources], coefficients[sources:])
+            yield
+            mixed = product(backward[...], kept)
+            yield
             if nyquist is None:
-                nyquist = real
+                nyquist = mixed[:sources]
                 continue
-            for part in range(2):
-                own_real, own_imag = real[:, columns(part)], imag[:, columns(part)]
-                moved = pltpu.roll(nyquist, HALF - group, 1) if group else nyquist
-                own_imag = jnp.where(lane_of_group == 0, moved, own_imag)
-                rows_of_group = slice(group * sources, (group + 1) * sources)
-                for half, value in enumerate((own_real, own_imag)):
-                    back[rows_of_group, columns(half)] = value.astype(jnp.bfloat16)
-                group += 1
+            pieces = []
+            for w in (first, first + 1):
+                real, imag = (
+                    mixed[part * sources : (part + 1) * sources, columns(w - first)]
+                    for part in range(2)
+                )
+                moved = pltpu.roll(nyquist, HALF - w, 1) if w else nyquist
+                imag = jnp.where(lane_of_group == 0, moved, imag)
+                pieces.append(jnp.concatenate([real, imag], axis=1).astype(jnp.bfloat16))
+            restored = product(jnp.concatenate(pieces, axis=0), inverse[...])
+            yield
+            if sweep < ITERS - 1:
+                start = (r * windows + first) * sources
+                estimates[start : start + 2 * sources, :] = restored.astype(jnp.bfloat16)
+            else:
+                deliver(r, first, restored)
+            yield
 
     def swapped(value):
         return pltpu.roll(value, SUB // 2, 1)
@@ -278,25 +296,31 @@
                 target = (2 * k + side) * blocks_of_time + block
                 out[target, r, inside * SUB : (inside + 2) * SUB, :] = both[k]
 
-    for sweep in range(ITERS):
-        update_and_forward_in_time(sweep)
-        shrink(sweep)
-        back_in_source()
-        for start in range(0, groups, SPAN):
-            rows_of_span = slice(start * sources, (start + SPAN) * sources)
-            restored = product(back[rows_of_span, :], inverse[...])
-            if sweep < ITERS - 1:
-                estimates[rows_of_span, :] = restored.astype(jnp.bfloat16)
-                continue
-            for group in range(0, SPAN, 2):
-                pair = restored[group * sources : (group + 2) * sources]
-                deliver((start + group) // windows, (start + group) % windows, pair)
-
-
-def cast_kernel(blended, delays, limits, sent, delays_near, limits_near):
-    sent[...] = blended[...].astype(jnp.bfloat16)
-    delays_near[...] = delays[...]
-    limits_near[...] = limits[...]
+    bounds = [bounds_of(sweep) for sweep in range(ITERS)]
+    turns = [(sweep, r) for sweep in range(ITERS) for r in range(receivers)]
+    interleaved(onward_steps(*turns[0]))
+    for before, after in zip(turns, turns[1:]):
+        if receivers > 1:
+            interleaved(onward_steps(*after), backward_steps(*before))
+        else:
+            interleaved(backward_steps(*before))
+            interleaved(onward_steps(*after))
+    interleaved(backward_steps(*turns[-1]))
+
+
+def cast_kernel(blended, sent, held, sems):
+    pieces = sems.shape[0]
+    count = blended.shape[0] // pieces
+    spans = [pl.ds(at * count, count) for at in range(pieces)]
+    copies = [
+        pltpu.make_async_copy(blended.at[span], held.at[span], sems.at[at])
+        for at, span in enumerate(spans)
+    ]
+    for copy in copies:
+        copy.start()
+    for copy, span in zip(copies, spans):
+        copy.wait()
+        sent[span] = held[span].astype(jnp.bfloat16)
 
 
 def gathers_of_all_samples(shots, blended, delays, thresholds):
@@ -310,18 +334,19 @@
     rows = blocks * own
     sent = blended.reshape(receivers, own, blocks, BLK).transpose(0, 2, 1, 3)
     sent = sent.reshape(count, each, rows, BLK)
-    vmem = pl.BlockSpec(memory_space=pltpu.VMEM)
-    sent, delays, thresholds = pl.pallas_call(
+    vmem, far = pl.BlockSpec(memory_space=pltpu.VMEM), pl.BlockSpec(memory_space=pl.ANY)
+
+    def kept_far(array):
+        return pltpu.with_memory_space_constraint(array, pltpu.HBM)
+
+    sent = pl.pallas_call(
         cast_kernel,
-        out_shape=(
-            jax.ShapeDtypeStruct(sent.shape, jnp.bfloat16),
-            jax.ShapeDtypeStruct(delays.T.shape, delays.dtype),
-            jax.ShapeDtypeStruct(thresholds.shape, thresholds.dtype),
-        ),
-        in_specs=[vmem] * 3,
-        out_specs=[vmem] * 3,
+        out_shape=jax.ShapeDtypeStruct(sent.shape, jnp.bfloat16),
+        in_specs=[far],
+        out_specs=vmem,
+        scratch_shapes=[pltpu.VMEM(sent.shape, jnp.float32), pltpu.SemaphoreType.DMA((4,))],
         compiler_params=pltpu.CompilerParams(vmem_limit_bytes=8 * 1024 * 1024),
-    )(sent, delays.T, thresholds)
+    )(kept_far(sent))
     received = lax.all_to_all(sent, ("shot", "tm"), split_axis=0, concat_axis=0, tiled=True)
     tables, limit_scale, kept_scale = half_spectrum_tables()
     tables = np.concatenate(tables[:2] + order_tables(windows, own) + tables[2:], axis=0)
@@ -329,17 +354,16 @@
     restored = pl.pallas_call(
         functools.partial(gather_kernel, shots, float(limit_scale), float(kept_scale)),
         out_shape=jax.ShapeDtypeStruct((count, each, blocks * held, BLK), jnp.bfloat16),
-        in_specs=[pl.BlockSpec(memory_space=pl.ANY)] + [vmem] * 3,
+        in_specs=[far] * 2 + [vmem] * 2,
         out_specs=vmem,
         scratch_shapes=[
-            pltpu.SMEM(delays.shape, jnp.int32),
+            pltpu.SMEM(delays.T.shape, jnp.int32),
+            pltpu.VMEM(thresholds.shape, jnp.float32),
             pltpu.VMEM((SRC * windows // TILE, TILE, each * BLK), jnp.float32),
-            pltpu.VMEM((4 * SRC, (groups + 1) * HALF), jnp.bfloat16),
-            pltpu.VMEM((4 * SRC, (groups + 1) * HALF), jnp.bfloat16),
+            pltpu.VMEM((each, 4 * SRC, (windows + 1) * HALF), jnp.bfloat16),
             pltpu.VMEM((groups * SRC, WIN), jnp.bfloat16),
             pltpu.VMEM((groups * SRC, WIN), jnp.bfloat16),
-            pltpu.VMEM((groups * SRC, WIN), jnp.bfloat16),
-            pltpu.SemaphoreType.DMA(()),
+            pltpu.SemaphoreType.DMA((2,)),
         ],
         compiler_params=pltpu.CompilerParams(vmem_limit_bytes=40 * 1024 * 1024),
         cost_estimate=pl.CostEstimate(
@@ -347,7 +371,7 @@
             bytes_accessed=2 * 1024 * 1024,
             transcendentals=ITERS * groups * SRC * HALF,
         ),
-    )(delays, thresholds, received, jnp.asarray(tables))
+    )(kept_far(delays.T), kept_far(thresholds), received, jnp.asarray(tables))
     final = lax.all_to_all(restored, ("shot", "tm"), split_axis=0, concat_axis=0, tiled=True)
     final = final.reshape(receivers, blocks, held, BLK).transpose(0, 2, 1, 3)
     return final.reshape(receivers, held, samples)

time: 43.3 us -> 45.4 us (1.048)
  Pallas kernels: 5 us -> 8.84 us
  local copies, waits for them, and re-layouts: 2.53 us -> 0.8 us
    pallas_call x1, Pallas kernels: 4.98 us -> 7.63 us  [gathers_of_all_samples(): pl.pallas_call(functools.partial(gather_kernel, shots, float(limit_scale)...]
    unnamed x9 -> x3, local copies, waits for them, and re-layouts: 2.53 us -> 0.8 us
    pallas_call x1, Pallas kernels: 0.03 us -> 1.21 us  [gathers_of_all_samples(): pl.pallas_call(cast_kernel, out_shape=jax.ShapeDtypeStruct(sent.shape, jn...]
where the time goes in v6:
time: 45.4 us; the launch traced here: 45.2 us
  blocking collectives  35.5 us (78%)
  Pallas kernels  8.84 us (19%)
  local copies, waits for them, and re-layouts  0.8 us (2%)
    all_to_all x1, blocking collectives, gathers_of_all_samples(): lax.all_to_all(restored, ('shot', 'tm'), split_axis=0, concat_axis=0, til...  18.1 us
    all_to_all x1, blocking collectives, gathers_of_all_samples(): lax.all_to_all(sent, ('shot', 'tm'), split_axis=0, concat_axis=0, tiled=T...  17.5 us
    pallas_call x1, Pallas kernels, gathers_of_all_samples(): pl.pallas_call(functools.partial(gather_kernel, shots, float(limit_scale)...  7.63 us
    pallas_call x1, Pallas kernels, gathers_of_all_samples(): pl.pallas_call(cast_kernel, out_shape=jax.ShapeDtypeStruct(sent.shape, jn...  1.21 us

profile of v6, /device:TPU:1, one launch (start us, length us, event | category | flops | bytes accessed | tf_op | source)
XLA Modules:
  0.0 45.2 jit_solution(12854824021298616271)
XLA Ops:
  0.0 0.0 copy-start
  0.0 1.2 %shard_map.46 = bf16[32,2,16,128]{3,2,1,0:T(8,128)(2,1)S(1)} custom-call(f32[32,2,16,128]{3,2,1,0:T(8,128)} %bitcast.12), custom_call_target="tpu_custom_call" | custom-call | tf_op jit(solution)/shard_map/pallas_call | solution.py:342
  1.2 17.5 %all_to_all.10.received = bf16[32,2,16,128]{3,2,1,0:T(8,128)(2,1)S(1)} all-to-all(bf16[32,2,16,128]{3,2,1,0:T(8,128)(2,1)S(1)} %shard_map.46), channel_id=1, replica_groups=mesh['shot'=16,'tm'=2] {'shot','tm'}, dimensions={0} | all-to-all | bytes 524288 | tf_op jit(solution)/shard_map/all_to_all | solution.py:350
  18.7 0.0 copy-done
  18.7 7.6 %shard_map.47 = bf16[32,2,32,128]{3,2,1,0:T(8,128)(2,1)S(1)} custom-call(s32[2,32]{1,0:T(2,128)} %bitcast.13, f32[2,64]{1,0:T(2,128)} %limits_far.1, bf16[32,2,16,128]{3,2,1,0:T(8,128)(2,1)S(1)} %all_to_all.10.received, bf16[1536,256]{1,0:T(8,128)(2,1)S(1)} %copy-done), custom_call_target="tpu_custom_call" | custom-call | flops 1342177280 | bytes 2097152 | tf_op jit(solution)/shard_map/pallas_call | solution.py:354
  26.3 18.1 %all_to_all.11 = bf16[32,2,32,128]{3,2,1,0:T(8,128)(2,1)S(1)} all-to-all(bf16[32,2,32,128]{3,2,1,0:T(8,128)(2,1)S(1)} %shard_map.47), channel_id=1, replica_groups=mesh['shot'=16,'tm'=2] {'shot','tm'}, dimensions={0} | all-to-all | bytes 1048576 | tf_op jit(solution)/shard_map/all_to_all | solution.py:375
  44.4 0.8 %copy.8 = bf16[64,4,1024]{2,1,0:T(4,128)(2,1)} copy(bf16[64,4,1024]{2,1,0:T(4,128)(2,1)S(1)} %bitcast.11) | data formatting | bytes 1048576
Async XLA Ops:
  0.0 18.7 %copy-start = (bf16[1536,256]{1,0:T(8,128)(2,1)S(1)}, bf16[1536,256]{1,0:T(8,128)(2,1)}, u32[]{:S(2)}) copy-start(bf16[1536,256]{1,0:T(8,128)(2,1)} %constant.2.clone.tables) | copy-start | bytes 2359300

commit v7 on v5

--- a/solution.py
+++ b/solution.py
@@ -20,7 +20,6 @@
 RELAX = 0.5
 HALF = WIN // 2
 SUB = 8
-SPAN = 4
 TILE = 256
 
 
@@ -119,10 +118,12 @@
     lane_of_group = lax.broadcasted_iota(jnp.int32, (sources, HALF), 1)
     lane_of_some = lax.broadcasted_iota(jnp.int32, (some, HALF), 1)
 
-    for chunk in range(sources // some):
-        senders = slice(chunk * TILE // rows, (chunk + 1) * TILE // rows)
-        arrived = [received[senders, r].reshape(TILE, BLK) for r in range(receivers)]
-        records[chunk] = product(order_arrived[...], jnp.concatenate(arrived, axis=1))
+    arrived = [
+        received[slice(chunk * TILE // rows, (chunk + 1) * TILE // rows), r].reshape(TILE, BLK)
+        for chunk in range(sources // some)
+        for r in range(receivers)
+    ]
+    records[...] = product(order_arrived[...], jnp.concatenate(arrived, axis=1))
 
     copy.wait()
 
@@ -145,14 +146,14 @@
             jnp.where(same, odd, jnp.where(ahead, other, even)),
         )
 
-    def columns(group, many=1):
-        return slice(group * HALF, (group + many) * HALF)
+    def columns(group):
+        return slice(group * HALF, (group + 1) * HALF)
 
     def first_update(r, chunk):
         updated = []
         for at in range(0, some, SRC_EXP):
             even, odd = (
-                records[chunk, pl.ds((at + half) * windows, windows), columns(r)]
+                records[pl.ds((at + half) * windows, windows), columns(chunk * receivers + r)]
                 for half in range(2)
             )
             for k in range(SRC_EXP):
@@ -162,12 +163,18 @@
         firsts[pl.ds((r * sources + chunk * some) * windows, TILE), :] = updated
         return updated
 
-    def later_update(r, chunk):
-        before = [
-            estimates[pl.ds((r * windows + w) * sources + chunk * some, some), :]
-            for w in range(windows)
-        ]
-        before = product(order_sources[...], jnp.concatenate(before, axis=0))
+    def side_by_side(values):
+        return jnp.concatenate(values, axis=1)
+
+    def estimates_by_source():
+        parts_of_rows = []
+        for r, chunk in turns:
+            starts = [(r * windows + w) * sources + chunk * some for w in range(windows)]
+            rows_of_part = [estimates[start : start + some, :] for start in starts]
+            parts_of_rows.append(jnp.concatenate(rows_of_part, axis=0))
+        return product(order_sources[...], side_by_side(parts_of_rows))
+
+    def later_update(r, chunk, before):
         first = (r * sources + chunk * some) * windows
         updated = []
         for at in range(0, some, SRC_EXP):
@@ -191,21 +198,30 @@
                 updated.append(jnp.concatenate([even, odd], axis=1) + step)
         return jnp.concatenate(updated, axis=0).astype(jnp.bfloat16)
 
+    turns = [(r, chunk) for r in range(receivers) for chunk in range(sources // some)]
+
     def update_and_forward_in_time(sweep):
+        if sweep:
+            before = estimates_by_source()
+            updates = [
+                later_update(r, chunk, before[:, at * WIN : (at + 1) * WIN])
+                for at, (r, chunk) in enumerate(turns)
+            ]
+        else:
+            updates = [first_update(r, chunk) for r, chunk in turns]
+        signal = product(order_windows[...], side_by_side(updates)).astype(jnp.bfloat16)
+        signal = [signal[:, at * WIN : (at + 1) * WIN] for at in range(len(turns))]
+        spectra = product(jnp.concatenate(signal, axis=0), forward[...])
         nyquists = [jnp.zeros((some, HALF), jnp.float32) for _ in range(sources // some)]
-        for r in range(receivers):
-            for chunk in range(sources // some):
-                update = later_update if sweep else first_update
-                signal = product(order_windows[...], update(r, chunk))
-                spectra = product(signal.astype(jnp.bfloat16), forward[...])
-                for w in range(windows):
-                    group = r * windows + w
-                    spectrum = spectra[w * some : (w + 1) * some]
-                    real, imag = spectrum[:, :HALF], spectrum[:, HALF:]
-                    moved = pltpu.roll(imag, group, 1) if group else imag
-                    nyquists[chunk] = jnp.where(lane_of_some == group, moved, nyquists[chunk])
-                    imag = jnp.where(lane_of_some == 0, 0.0, imag)
-                    put(field, columns(group), real, imag, chunk * some)
+        for at, (r, chunk) in enumerate(turns):
+            for w in range(windows):
+                group = r * windows + w
+                start = at * TILE + w * some
+                real, imag = (spectra[start : start + some, columns(half)] for half in range(2))
+                moved = pltpu.roll(imag, group, 1) if group else imag
+                nyquists[chunk] = jnp.where(lane_of_some == group, moved, nyquists[chunk])
+                imag = jnp.where(lane_of_some == 0, 0.0, imag)
+                put(field, columns(group), real, imag, chunk * some)
         for chunk, nyquist in enumerate(nyquists):
             put(field, columns(groups), nyquist, jnp.zeros_like(nyquist), chunk * some)
 
@@ -216,13 +232,8 @@
             start = at * sources + first
             ref[start : start + value.shape[0], where] = value
 
-    def chunks():
-        yield columns(groups)
-        for group in range(0, groups, 2):
-            yield columns(group, 2)
-
-    def mixing(table, ref, where):
-        total = product(table[...], ref[:, where])
+    def mixing(table, ref):
+        total = product(table[...], ref[...])
         return total[:sources], total[sources:]
 
     def shrink(sweep):
@@ -232,30 +243,22 @@
         bound = jnp.sum(jnp.where(p == q, limit, 0.0), axis=1, keepdims=True)
         mirrored = (p + q == 0) | (p + q == sources)
         bound_mirrored = jnp.sum(jnp.where(mirrored, limit, 0.0), axis=1, keepdims=True)
-        for where in chunks():
-            real, imag = mixing(onward, field, where)
-            inverse_size = lax.rsqrt(real * real + imag * imag)
-            factor = jnp.maximum(kept_scale - bound * inverse_size, 0.0) + jnp.maximum(
-                kept_scale - bound_mirrored * inverse_size, 0.0
-            )
-            put(mixed, where, real * factor, imag * factor)
+        real, imag = mixing(onward, field)
+        inverse_size = lax.rsqrt(real * real + imag * imag)
+        factor = jnp.maximum(kept_scale - bound * inverse_size, 0.0) + jnp.maximum(
+            kept_scale - bound_mirrored * inverse_size, 0.0
+        )
+        put(mixed, slice(None), real * factor, imag * factor)
 
     def back_in_source():
-        nyquist = None
-        group = 0
-        for where in chunks():
-            real, imag = mixing(backward, mixed, where)
-            if nyquist is None:
-                nyquist = real
-                continue
-            for part in range(2):
-                own_real, own_imag = real[:, columns(part)], imag[:, columns(part)]
-                moved = pltpu.roll(nyquist, HALF - group, 1) if group else nyquist
-                own_imag = jnp.where(lane_of_group == 0, moved, own_imag)
-                rows_of_group = slice(group * sources, (group + 1) * sources)
-                for half, value in enumerate((own_real, own_imag)):
-                    back[rows_of_group, columns(half)] = value.astype(jnp.bfloat16)
-                group += 1
+        real, imag = mixing(backward, mixed)
+        nyquist = real[:, columns(groups)]
+        for group in range(groups):
+            moved = pltpu.roll(nyquist, HALF - group, 1) if group else nyquist
+            own_imag = jnp.where(lane_of_group == 0, moved, imag[:, columns(group)])
+            rows_of_group = slice(group * sources, (group + 1) * sources)
+            for half, value in enumerate((real[:, columns(group)], own_imag)):
+                back[rows_of_group, columns(half)] = value.astype(jnp.bfloat16)
 
     def swapped(value):
         return pltpu.roll(value, SUB // 2, 1)
@@ -282,21 +285,34 @@
         update_and_forward_in_time(sweep)
         shrink(sweep)
         back_in_source()
-        for start in range(0, groups, SPAN):
-            rows_of_span = slice(start * sources, (start + SPAN) * sources)
-            restored = product(back[rows_of_span, :], inverse[...])
-            if sweep < ITERS - 1:
-                estimates[rows_of_span, :] = restored.astype(jnp.bfloat16)
-                continue
-            for group in range(0, SPAN, 2):
-                pair = restored[group * sources : (group + 2) * sources]
-                deliver((start + group) // windows, (start + group) % windows, pair)
-
-
-def cast_kernel(blended, delays, limits, sent, delays_near, limits_near):
-    sent[...] = blended[...].astype(jnp.bfloat16)
-    delays_near[...] = delays[...]
-    limits_near[...] = limits[...]
+        restored = product(back[...], inverse[...])
+        if sweep < ITERS - 1:
+            estimates[...] = restored.astype(jnp.bfloat16)
+            continue
+        for group in range(0, groups, 2):
+            pair = restored[group * sources : (group + 2) * sources]
+            deliver(group // windows, group % windows, pair)
+
+
+def cast_kernel(blended, delays, limits, sent, delays_near, limits_near, held, sems):
+    pieces = sems.shape[0] - 2
+    count = blended.shape[0] // pieces
+    spans = [pl.ds(at * count, count) for at in range(pieces)]
+    copies = [
+        pltpu.make_async_copy(blended.at[span], held.at[span], sems.at[at])
+        for at, span in enumerate(spans)
+    ]
+    small = [
+        pltpu.make_async_copy(delays, delays_near, sems.at[pieces]),
+        pltpu.make_async_copy(limits, limits_near, sems.at[pieces + 1]),
+    ]
+    for copy in copies + small:
+        copy.start()
+    for copy, span in zip(copies, spans):
+        copy.wait()
+        sent[span] = held[span].astype(jnp.bfloat16)
+    for copy in small:
+        copy.wait()
 
 
 def gathers_of_all_samples(shots, blended, delays, thresholds):
@@ -310,7 +326,11 @@
     rows = blocks * own
     sent = blended.reshape(receivers, own, blocks, BLK).transpose(0, 2, 1, 3)
     sent = sent.reshape(count, each, rows, BLK)
-    vmem = pl.BlockSpec(memory_space=pltpu.VMEM)
+    vmem, far = pl.BlockSpec(memory_space=pltpu.VMEM), pl.BlockSpec(memory_space=pl.ANY)
+
+    def kept_far(array):
+        return pltpu.with_memory_space_constraint(array, pltpu.HBM)
+
     sent, delays, thresholds = pl.pallas_call(
         cast_kernel,
         out_shape=(
@@ -318,10 +338,14 @@
             jax.ShapeDtypeStruct(delays.T.shape, delays.dtype),
             jax.ShapeDtypeStruct(thresholds.shape, thresholds.dtype),
         ),
-        in_specs=[vmem] * 3,
+        in_specs=[far] * 3,
         out_specs=[vmem] * 3,
+        scratch_shapes=[
+            pltpu.VMEM(sent.shape, jnp.float32),
+            pltpu.SemaphoreType.DMA((4 + 2,)),
+        ],
         compiler_params=pltpu.CompilerParams(vmem_limit_bytes=8 * 1024 * 1024),
-    )(sent, delays.T, thresholds)
+    )(kept_far(sent), kept_far(delays.T), kept_far(thresholds))
     received = lax.all_to_all(sent, ("shot", "tm"), split_axis=0, concat_axis=0, tiled=True)
     tables, limit_scale, kept_scale = half_spectrum_tables()
     tables = np.concatenate(tables[:2] + order_tables(windows, own) + tables[2:], axis=0)
@@ -333,7 +357,7 @@
         out_specs=vmem,
         scratch_shapes=[
             pltpu.SMEM(delays.shape, jnp.int32),
-            pltpu.VMEM((SRC * windows // TILE, TILE, each * BLK), jnp.float32),
+            pltpu.VMEM((TILE, SRC * windows // TILE * each * BLK), jnp.float32),
             pltpu.VMEM((4 * SRC, (groups + 1) * HALF), jnp.bfloat16),
             pltpu.VMEM((4 * SRC, (groups + 1) * HALF), jnp.bfloat16),
             pltpu.VMEM((groups * SRC, WIN), jnp.bfloat16),

time: 43.3 us -> 42.3 us (0.977)
  local copies, waits for them, and re-layouts: 2.53 us -> 0.8 us
  Pallas kernels: 5 us -> 5.72 us
    unnamed x9 -> x3, local copies, waits for them, and re-layouts: 2.53 us -> 0.8 us
    pallas_call x1, Pallas kernels: 0.03 us -> 1.23 us  [gathers_of_all_samples(): pl.pallas_call(cast_kernel, out_shape=(jax.ShapeDtypeStruct(sent.shape, j...]
    pallas_call x1, Pallas kernels: 4.98 us -> 4.49 us  [gathers_of_all_samples(): pl.pallas_call(functools.partial(gather_kernel, shots, float(limit_scale)...]
where the time goes in v7:
time: 42.3 us; the launch traced here: 42.1 us
  blocking collectives  35.5 us (84%)
  Pallas kernels  5.72 us (14%)
  local copies, waits for them, and re-layouts  0.8 us (2%)
    all_to_all x1, blocking collectives, gathers_of_all_samples(): lax.all_to_all(restored, ('shot', 'tm'), split_axis=0, concat_axis=0, til...  18.1 us
    all_to_all x1, blocking collectives, gathers_of_all_samples(): lax.all_to_all(sent, ('shot', 'tm'), split_axis=0, concat_axis=0, tiled=T...  17.5 us
    pallas_call x1, Pallas kernels, gathers_of_all_samples(): pl.pallas_call(functools.partial(gather_kernel, shots, float(limit_scale)...  4.49 us
    pallas_call x1, Pallas kernels, gathers_of_all_samples(): pl.pallas_call(cast_kernel, out_shape=(jax.ShapeDtypeStruct(sent.shape, j...  1.23 us

profile of v7, /device:TPU:1, one launch (start us, length us, event | category | flops | bytes accessed | tf_op | source)
XLA Modules:
  0.0 42.1 jit_solution(5176714800040004142)
XLA Ops:
  0.0 0.0 copy-start
  0.0 1.2 %shard_map.46 = (bf16[32,2,16,128]{3,2,1,0:T(8,128)(2,1)S(1)}, s32[2,32]{1,0:T(2,128)S(1)}, f32[2,64]{1,0:T(2,128)S(1)}) custom-call(f32[32,2,16,128]{3,2,1,0:T(8,128)} %bitcast.12, s32[2,32]{1,0:T(2,128)} %bitcast.13, f32[2,64]{1,0:T(2,128)} %limits.1), custom_call_target="tpu_custom_call" | custom-call | tf_op jit(solution)/shard_map/pallas_call | solution.py:334
  1.2 17.5 %all_to_all.10.received = bf16[32,2,16,128]{3,2,1,0:T(8,128)(2,1)S(1)} all-to-all(bf16[32,2,16,128]{3,2,1,0:T(8,128)(2,1)S(1)} %get-tuple-element.10), channel_id=1, replica_groups=mesh['shot'=16,'tm'=2] {'shot','tm'}, dimensions={0} | all-to-all | bytes 524288 | tf_op jit(solution)/shard_map/all_to_all | solution.py:349
  18.7 0.0 copy-done
  18.7 4.5 %shard_map.47 = bf16[32,2,32,128]{3,2,1,0:T(8,128)(2,1)S(1)} custom-call(s32[2,32]{1,0:T(2,128)S(1)} %get-tuple-element.8.delays_far, f32[2,64]{1,0:T(2,128)S(1)} %get-tuple-element.9.limits, bf16[32,2,16,128]{3,2,1,0:T(8,128)(2,1)S(1)} %all_to_all.10.received, bf16[1536,256]{1,0:T(8,128)(2,1)S(1)} %copy-done), custom_call_target="tpu_custom_call" | custom-call | flops 1342177280 | bytes 2097152 | tf_op jit(solution)/shard_map/pallas_call | solution.py:353
  23.2 18.1 %all_to_all.11 = bf16[32,2,32,128]{3,2,1,0:T(8,128)(2,1)S(1)} all-to-all(bf16[32,2,32,128]{3,2,1,0:T(8,128)(2,1)S(1)} %shard_map.47), channel_id=1, replica_groups=mesh['shot'=16,'tm'=2] {'shot','tm'}, dimensions={0} | all-to-all | bytes 1048576 | tf_op jit(solution)/shard_map/all_to_all | solution.py:375
  41.3 0.8 %copy.8 = bf16[64,4,1024]{2,1,0:T(4,128)(2,1)} copy(bf16[64,4,1024]{2,1,0:T(4,128)(2,1)S(1)} %bitcast.11) | data formatting | bytes 1048576
Async XLA Ops:
  0.0 18.7 %copy-start = (bf16[1536,256]{1,0:T(8,128)(2,1)S(1)}, bf16[1536,256]{1,0:T(8,128)(2,1)}, u32[]{:S(2)}) copy-start(bf16[1536,256]{1,0:T(8,128)(2,1)} %constant.2.clone.tables) | copy-start | bytes 2359300

commit v8 on v7

--- a/solution.py
+++ b/solution.py
@@ -243,12 +243,14 @@
         bound = jnp.sum(jnp.where(p == q, limit, 0.0), axis=1, keepdims=True)
         mirrored = (p + q == 0) | (p + q == sources)
         bound_mirrored = jnp.sum(jnp.where(mirrored, limit, 0.0), axis=1, keepdims=True)
-        real, imag = mixing(onward, field)
-        inverse_size = lax.rsqrt(real * real + imag * imag)
-        factor = jnp.maximum(kept_scale - bound * inverse_size, 0.0) + jnp.maximum(
-            kept_scale - bound_mirrored * inverse_size, 0.0
-        )
-        put(mixed, slice(None), real * factor, imag * factor)
+        all_real, all_imag = mixing(onward, field)
+        for group in range(groups + 1):
+            real, imag = all_real[:, columns(group)], all_imag[:, columns(group)]
+            inverse_size = lax.rsqrt(real * real + imag * imag)
+            factor = jnp.maximum(kept_scale - bound * inverse_size, 0.0) + jnp.maximum(
+                kept_scale - bound_mirrored * inverse_size, 0.0
+            )
+            put(mixed, columns(group), real * factor, imag * factor)
 
     def back_in_source():
         real, imag = mixing(backward, mixed)
@@ -306,7 +308,7 @@
         pltpu.make_async_copy(delays, delays_near, sems.at[pieces]),
         pltpu.make_async_copy(limits, limits_near, sems.at[pieces + 1]),
     ]
-    for copy in copies + small:
+    for copy in small + copies:
         copy.start()
     for copy, span in zip(copies, spans):
         copy.wait()

time: 42.3 us -> 42.5 us (level)
  no operation moved by 1% of the time
where the time goes in v8:
time: 42.5 us; the launch traced here: 42.3 us
  blocking collectives  35.5 us (84%)
  Pallas kernels  5.94 us (14%)
  local copies, waits for them, and re-layouts  0.8 us (2%)
    all_to_all x1, blocking collectives, gathers_of_all_samples(): lax.all_to_all(restored, ('shot', 'tm'), split_axis=0, concat_axis=0, til...  18.1 us
    all_to_all x1, blocking collectives, gathers_of_all_samples(): lax.all_to_all(sent, ('shot', 'tm'), split_axis=0, concat_axis=0, tiled=T...  17.5 us
    pallas_call x1, Pallas kernels, gathers_of_all_samples(): pl.pallas_call(functools.partial(gather_kernel, shots, float(limit_scale)...  4.68 us
    pallas_call x1, Pallas kernels, gathers_of_all_samples(): pl.pallas_call(cast_kernel, out_shape=(jax.ShapeDtypeStruct(sent.shape, j...  1.26 us

profile of v8, /device:TPU:1, one launch (start us, length us, event | category | flops | bytes accessed | tf_op | source)
XLA Modules:
  0.0 42.3 jit_solution(16559883854396813862)
XLA Ops:
  0.0 0.0 copy-start
  0.0 1.3 %shard_map.46 = (bf16[32,2,16,128]{3,2,1,0:T(8,128)(2,1)S(1)}, s32[2,32]{1,0:T(2,128)S(1)}, f32[2,64]{1,0:T(2,128)S(1)}) custom-call(f32[32,2,16,128]{3,2,1,0:T(8,128)} %bitcast.12, s32[2,32]{1,0:T(2,128)} %bitcast.13, f32[2,64]{1,0:T(2,128)} %limits.1), custom_call_target="tpu_custom_call" | custom-call | tf_op jit(solution)/shard_map/pallas_call | solution.py:336
  1.3 17.5 %all_to_all.10.received = bf16[32,2,16,128]{3,2,1,0:T(8,128)(2,1)S(1)} all-to-all(bf16[32,2,16,128]{3,2,1,0:T(8,128)(2,1)S(1)} %get-tuple-element.10), channel_id=1, replica_groups=mesh['shot'=16,'tm'=2] {'shot','tm'}, dimensions={0} | all-to-all | bytes 524288 | tf_op jit(solution)/shard_map/all_to_all | solution.py:351
  18.7 0.0 copy-done
  18.7 4.7 %shard_map.47 = bf16[32,2,32,128]{3,2,1,0:T(8,128)(2,1)S(1)} custom-call(s32[2,32]{1,0:T(2,128)S(1)} %get-tuple-element.8.delays_far, f32[2,64]{1,0:T(2,128)S(1)} %get-tuple-element.9.limits, bf16[32,2,16,128]{3,2,1,0:T(8,128)(2,1)S(1)} %all_to_all.10.received, bf16[1536,256]{1,0:T(8,128)(2,1)S(1)} %copy-done), custom_call_target="tpu_custom_call" | custom-call | flops 1342177280 | bytes 2097152 | tf_op jit(solution)/shard_map/pallas_call | solution.py:355
  23.4 18.1 %all_to_all.11 = bf16[32,2,32,128]{3,2,1,0:T(8,128)(2,1)S(1)} all-to-all(bf16[32,2,32,128]{3,2,1,0:T(8,128)(2,1)S(1)} %shard_map.47), channel_id=1, replica_groups=mesh['shot'=16,'tm'=2] {'shot','tm'}, dimensions={0} | all-to-all | bytes 1048576 | tf_op jit(solution)/shard_map/all_to_all | solution.py:377
  41.5 0.8 %copy.8 = bf16[64,4,1024]{2,1,0:T(4,128)(2,1)} copy(bf16[64,4,1024]{2,1,0:T(4,128)(2,1)S(1)} %bitcast.11) | data formatting | bytes 1048576
Async XLA Ops:
  0.0 18.7 %copy-start = (bf16[1536,256]{1,0:T(8,128)(2,1)S(1)}, bf16[1536,256]{1,0:T(8,128)(2,1)}, u32[]{:S(2)}) copy-start(bf16[1536,256]{1,0:T(8,128)(2,1)} %constant.2.clone.tables) | copy-start | bytes 2359300

commit v9 on v7

--- a/solution.py
+++ b/solution.py
@@ -45,16 +45,16 @@
     turn = (source[:, None] * source[None, :] % SRC) * (2.0 * math.pi / SRC)
     cosine, sine = np.cos(turn) / math.sqrt(SRC), np.sin(turn) / math.sqrt(SRC)
     onward = np.block([[cosine, sine], [-sine, cosine]])
-    source_scale, time_scale = bfloat_scale(onward), bfloat_scale(inverse)
-    onward = onward * source_scale
-    tables = (
-        forward,
-        inverse * time_scale,
-        np.concatenate([onward, onward], axis=1) / math.sqrt(WIN),
-        np.concatenate([onward.T, onward.T], axis=1),
-    )
-    tables = tuple(table.astype(ml_dtypes.bfloat16) for table in tables)
-    return tables, source_scale, 1.0 / (source_scale * source_scale * time_scale)
+    time_scale = bfloat_scale(inverse)
+    forward, inverse = (x.astype(ml_dtypes.bfloat16) for x in (forward, inverse * time_scale))
+    tables = forward, inverse, high_and_low(onward / math.sqrt(WIN)), high_and_low(onward.T)
+    return tables, 1.0 / time_scale
+
+
+def high_and_low(table):
+    high = table.astype(ml_dtypes.bfloat16)
+    low = (table - high.astype(np.float64)).astype(ml_dtypes.bfloat16)
+    return np.concatenate([high, low], axis=1)
 
 
 def rearranging(shape, axes):
@@ -71,18 +71,12 @@
     )
 
 
-def halves(value):
-    high = value.astype(jnp.bfloat16)
-    return high, (value - high.astype(jnp.float32)).astype(jnp.bfloat16)
-
-
 def product(left, right):
     return jnp.dot(left, right, preferred_element_type=jnp.float32)
 
 
 def gather_kernel(
     shots,
-    limit_scale,
     kept_scale,
     delays_far,
     limits,
@@ -226,18 +220,17 @@
             put(field, columns(groups), nyquist, jnp.zeros_like(nyquist), chunk * some)
 
     def put(ref, where, real, imag, first=0):
-        real_high, real_low = halves(real)
-        imag_high, imag_low = halves(imag)
-        for at, value in enumerate((real_high, imag_high, real_low, imag_low)):
+        for at, value in enumerate((real, imag)):
             start = at * sources + first
-            ref[start : start + value.shape[0], where] = value
+            ref[start : start + value.shape[0], where] = value.astype(jnp.bfloat16)
 
     def mixing(table, ref):
-        total = product(table[...], ref[...])
+        values = ref[...]
+        total = product(table[...], jnp.concatenate([values, values], axis=0))
         return total[:sources], total[sources:]
 
     def shrink(sweep):
-        limit = limits[sweep : sweep + 1, :] * (limit_scale * kept_scale)
+        limit = limits[sweep : sweep + 1, :] * kept_scale
         p = lax.broadcasted_iota(jnp.int32, (sources, sources), 0)
         q = lax.broadcasted_iota(jnp.int32, (sources, sources), 1)
         bound = jnp.sum(jnp.where(p == q, limit, 0.0), axis=1, keepdims=True)
@@ -347,19 +340,19 @@
         compiler_params=pltpu.CompilerParams(vmem_limit_bytes=8 * 1024 * 1024),
     )(kept_far(sent), kept_far(delays.T), kept_far(thresholds))
     received = lax.all_to_all(sent, ("shot", "tm"), split_axis=0, concat_axis=0, tiled=True)
-    tables, limit_scale, kept_scale = half_spectrum_tables()
+    tables, kept_scale = half_spectrum_tables()
     tables = np.concatenate(tables[:2] + order_tables(windows, own) + tables[2:], axis=0)
     held = SRC // shots
     restored = pl.pallas_call(
-        functools.partial(gather_kernel, shots, float(limit_scale), float(kept_scale)),
+        functools.partial(gather_kernel, shots, float(kept_scale)),
         out_shape=jax.ShapeDtypeStruct((count, each, blocks * held, BLK), jnp.bfloat16),
         in_specs=[pl.BlockSpec(memory_space=pl.ANY)] + [vmem] * 3,
         out_specs=vmem,
         scratch_shapes=[
             pltpu.SMEM(delays.shape, jnp.int32),
             pltpu.VMEM((TILE, SRC * windows // TILE * each * BLK), jnp.float32),
-            pltpu.VMEM((4 * SRC, (groups + 1) * HALF), jnp.bfloat16),
-            pltpu.VMEM((4 * SRC, (groups + 1) * HALF), jnp.bfloat16),
+            pltpu.VMEM((2 * SRC, (groups + 1) * HALF), jnp.bfloat16),
+            pltpu.VMEM((2 * SRC, (groups + 1) * HALF), jnp.bfloat16),
             pltpu.VMEM((groups * SRC, WIN), jnp.bfloat16),
             pltpu.VMEM((groups * SRC, WIN), jnp.bfloat16),
             pltpu.VMEM((groups * SRC, WIN), jnp.bfloat16),

time: 42.3 us -> 41.9 us (level)
  no operation moved by 1% of the time
where the time goes in v9:
time: 41.9 us; the launch traced here: 41.7 us
  blocking collectives  35.5 us (85%)
  Pallas kernels  5.4 us (13%)
  local copies, waits for them, and re-layouts  0.8 us (2%)
    all_to_all x1, blocking collectives, gathers_of_all_samples(): lax.all_to_all(restored, ('shot', 'tm'), split_axis=0, concat_axis=0, til...  18.1 us
    all_to_all x1, blocking collectives, gathers_of_all_samples(): lax.all_to_all(sent, ('shot', 'tm'), split_axis=0, concat_axis=0, tiled=T...  17.5 us
    pallas_call x1, Pallas kernels, gathers_of_all_samples(): pl.pallas_call(functools.partial(gather_kernel, shots, float(kept_scale))...  4.17 us
    pallas_call x1, Pallas kernels, gathers_of_all_samples(): pl.pallas_call(cast_kernel, out_shape=(jax.ShapeDtypeStruct(sent.shape, j...  1.23 us

profile of v9, /device:TPU:1, one launch (start us, length us, event | category | flops | bytes accessed | tf_op | source)
XLA Modules:
  0.0 41.7 jit_solution(13897449917376106504)
XLA Ops:
  0.0 0.0 copy-start
  0.0 1.2 %shard_map.46 = (bf16[32,2,16,128]{3,2,1,0:T(8,128)(2,1)S(1)}, s32[2,32]{1,0:T(2,128)S(1)}, f32[2,64]{1,0:T(2,128)S(1)}) custom-call(f32[32,2,16,128]{3,2,1,0:T(8,128)} %bitcast.12, s32[2,32]{1,0:T(2,128)} %bitcast.13, f32[2,64]{1,0:T(2,128)} %limits.1), custom_call_target="tpu_custom_call" | custom-call | tf_op jit(solution)/shard_map/pallas_call | solution.py:327
  1.2 17.5 %all_to_all.10.received = bf16[32,2,16,128]{3,2,1,0:T(8,128)(2,1)S(1)} all-to-all(bf16[32,2,16,128]{3,2,1,0:T(8,128)(2,1)S(1)} %get-tuple-element.10), channel_id=1, replica_groups=mesh['shot'=16,'tm'=2] {'shot','tm'}, dimensions={0} | all-to-all | bytes 524288 | tf_op jit(solution)/shard_map/all_to_all | solution.py:342
  18.7 0.0 copy-done
  18.7 4.2 %shard_map.47 = bf16[32,2,32,128]{3,2,1,0:T(8,128)(2,1)S(1)} custom-call(s32[2,32]{1,0:T(2,128)S(1)} %get-tuple-element.8.delays_far, f32[2,64]{1,0:T(2,128)S(1)} %get-tuple-element.9.limits, bf16[32,2,16,128]{3,2,1,0:T(8,128)(2,1)S(1)} %all_to_all.10.received, bf16[1536,256]{1,0:T(8,128)(2,1)S(1)} %copy-done), custom_call_target="tpu_custom_call" | custom-call | flops 1342177280 | bytes 2097152 | tf_op jit(solution)/shard_map/pallas_call | solution.py:346
  22.9 18.1 %all_to_all.11 = bf16[32,2,32,128]{3,2,1,0:T(8,128)(2,1)S(1)} all-to-all(bf16[32,2,32,128]{3,2,1,0:T(8,128)(2,1)S(1)} %shard_map.47), channel_id=1, replica_groups=mesh['shot'=16,'tm'=2] {'shot','tm'}, dimensions={0} | all-to-all | bytes 1048576 | tf_op jit(solution)/shard_map/all_to_all | solution.py:368
  41.0 0.8 %copy.8 = bf16[64,4,1024]{2,1,0:T(4,128)(2,1)} copy(bf16[64,4,1024]{2,1,0:T(4,128)(2,1)S(1)} %bitcast.11) | data formatting | bytes 1048576
Async XLA Ops:
  0.0 18.7 %copy-start = (bf16[1536,256]{1,0:T(8,128)(2,1)S(1)}, bf16[1536,256]{1,0:T(8,128)(2,1)}, u32[]{:S(2)}) copy-start(bf16[1536,256]{1,0:T(8,128)(2,1)} %constant.2.clone.tables) | copy-start | bytes 2359300

commit v10 on v9

--- a/solution.py
+++ b/solution.py
@@ -62,10 +62,12 @@
     return np.eye(order.size)[order].astype(ml_dtypes.bfloat16)
 
 
-def order_tables(windows, own):
+def order_tables(windows, own, blocks_of_time):
     shots, sources = TILE // (2 * windows * own), TILE // windows
     return (
-        rearranging((shots, windows, 2, own), (0, 3, 2, 1)),
+        rearranging(
+            (blocks_of_time, shots, windows // blocks_of_time, 2, own), (1, 4, 3, 0, 2)
+        ),
         rearranging((sources, windows), (1, 0)),
         rearranging((windows, sources), (1, 0)),
     )
@@ -112,8 +114,25 @@
     lane_of_group = lax.broadcasted_iota(jnp.int32, (sources, HALF), 1)
     lane_of_some = lax.broadcasted_iota(jnp.int32, (some, HALF), 1)
 
+    senders = TILE // (rows * blocks_of_time)
+    bounds = []
+    for sweep in range(ITERS):
+        limit = limits[sweep : sweep + 1, :] * kept_scale
+        p = lax.broadcasted_iota(jnp.int32, (sources, sources), 0)
+        q = lax.broadcasted_iota(jnp.int32, (sources, sources), 1)
+        bound = jnp.sum(jnp.where(p == q, limit, 0.0), axis=1, keepdims=True)
+        mirrored = (p + q == 0) | (p + q == sources)
+        bound_mirrored = jnp.sum(jnp.where(mirrored, limit, 0.0), axis=1, keepdims=True)
+        bounds.append((bound, bound_mirrored))
+
     arrived = [
-        received[slice(chunk * TILE // rows, (chunk + 1) * TILE // rows), r].reshape(TILE, BLK)
+        jnp.concatenate(
+            [
+                received[pl.ds(block * shots + chunk * senders, senders), r].reshape(-1, BLK)
+                for block in range(blocks_of_time)
+            ],
+            axis=0,
+        )
         for chunk in range(sources // some)
         for r in range(receivers)
     ]
@@ -230,12 +249,7 @@
         return total[:sources], total[sources:]
 
     def shrink(sweep):
-        limit = limits[sweep : sweep + 1, :] * kept_scale
-        p = lax.broadcasted_iota(jnp.int32, (sources, sources), 0)
-        q = lax.broadcasted_iota(jnp.int32, (sources, sources), 1)
-        bound = jnp.sum(jnp.where(p == q, limit, 0.0), axis=1, keepdims=True)
-        mirrored = (p + q == 0) | (p + q == sources)
-        bound_mirrored = jnp.sum(jnp.where(mirrored, limit, 0.0), axis=1, keepdims=True)
+        bound, bound_mirrored = bounds[sweep]
         real, imag = mixing(onward, field)
         inverse_size = lax.rsqrt(real * real + imag * imag)
         factor = jnp.maximum(kept_scale - bound * inverse_size, 0.0) + jnp.maximum(
@@ -271,7 +285,7 @@
             both = jnp.concatenate([pieces[0][side], pieces[1][side]], axis=1)
             both = both.astype(jnp.bfloat16)
             for k in range(sources // SUB):
-                target = (2 * k + side) * blocks_of_time + block
+                target = block * shots + 2 * k + side
                 out[target, r, inside * SUB : (inside + 2) * SUB, :] = both[k]
 
     for sweep in range(ITERS):
@@ -335,13 +349,13 @@
         out_specs=[vmem] * 3,
         scratch_shapes=[
             pltpu.VMEM(sent.shape, jnp.float32),
-            pltpu.SemaphoreType.DMA((4 + 2,)),
+            pltpu.SemaphoreType.DMA((1 + 2,)),
         ],
         compiler_params=pltpu.CompilerParams(vmem_limit_bytes=8 * 1024 * 1024),
     )(kept_far(sent), kept_far(delays.T), kept_far(thresholds))
-    received = lax.all_to_all(sent, ("shot", "tm"), split_axis=0, concat_axis=0, tiled=True)
+    received = lax.all_to_all(sent, ("tm", "shot"), split_axis=0, concat_axis=0, tiled=True)
     tables, kept_scale = half_spectrum_tables()
-    tables = np.concatenate(tables[:2] + order_tables(windows, own) + tables[2:], axis=0)
+    tables = np.concatenate(tables[:2] + order_tables(windows, own, blocks_of_time) + tables[2:], axis=0)
     held = SRC // shots
     restored = pl.pallas_call(
         functools.partial(gather_kernel, shots, float(kept_scale)),
@@ -365,7 +379,7 @@
             transcendentals=ITERS * groups * SRC * HALF,
         ),
     )(delays, thresholds, received, jnp.asarray(tables))
-    final = lax.all_to_all(restored, ("shot", "tm"), split_axis=0, concat_axis=0, tiled=True)
+    final = lax.all_to_all(restored, ("tm", "shot"), split_axis=0, concat_axis=0, tiled=True)
     final = final.reshape(receivers, blocks, held, BLK).transpose(0, 2, 1, 3)
     return final.reshape(receivers, held, samples)
 

time: 41.9 us -> 41.9 us (level)
  the two profiles are of different devices: /device:TPU:1 before, /device:TPU:0 now
where the time goes in v10:
time: 41.9 us; the launch traced here: 41.7 us
  blocking collectives  35.6 us (85%)
  Pallas kernels  5.26 us (13%)
  local copies, waits for them, and re-layouts  0.8 us (2%)
    all_to_all x1, blocking collectives, gathers_of_all_samples(): lax.all_to_all(restored, ('tm', 'shot'), split_axis=0, concat_axis=0, til...  18.2 us
    all_to_all x1, blocking collectives, gathers_of_all_samples(): lax.all_to_all(sent, ('tm', 'shot'), split_axis=0, concat_axis=0, tiled=T...  17.4 us
    pallas_call x1, Pallas kernels, gathers_of_all_samples(): pl.pallas_call(functools.partial(gather_kernel, shots, float(kept_scale))...  4.09 us
    pallas_call x1, Pallas kernels, gathers_of_all_samples(): pl.pallas_call(cast_kernel, out_shape=(jax.ShapeDtypeStruct(sent.shape, j...  1.17 us

profile of v10, /device:TPU:0, one launch (start us, length us, event | category | flops | bytes accessed | tf_op | source)
XLA Modules:
  0.0 41.7 jit_solution(9966271965216277849)
XLA Ops:
  0.0 0.0 copy-start
  0.0 1.2 %shard_map.46 = (bf16[32,2,16,128]{3,2,1,0:T(8,128)(2,1)S(1)}, s32[2,32]{1,0:T(2,128)S(1)}, f32[2,64]{1,0:T(2,128)S(1)}) custom-call(f32[32,2,16,128]{3,2,1,0:T(8,128)} %bitcast.12, s32[2,32]{1,0:T(2,128)} %bitcast.13, f32[2,64]{1,0:T(2,128)} %limits.1), custom_call_target="tpu_custom_call" | custom-call | tf_op jit(solution)/shard_map/pallas_call | solution.py:341
  1.2 17.4 %all_to_all.10.received = bf16[32,2,16,128]{3,2,1,0:T(8,128)(2,1)S(1)} all-to-all(bf16[32,2,16,128]{3,2,1,0:T(8,128)(2,1)S(1)} %get-tuple-element.10), channel_id=1, replica_groups=mesh['shot'=16,'tm'=2] {'tm','shot'}, dimensions={0} | all-to-all | bytes 524288 | tf_op jit(solution)/shard_map/all_to_all | solution.py:356
  18.6 0.0 copy-done
  18.6 4.1 %shard_map.47 = bf16[32,2,32,128]{3,2,1,0:T(8,128)(2,1)S(1)} custom-call(s32[2,32]{1,0:T(2,128)S(1)} %get-tuple-element.8.delays_far, f32[2,64]{1,0:T(2,128)S(1)} %get-tuple-element.9.limits, bf16[32,2,16,128]{3,2,1,0:T(8,128)(2,1)S(1)} %all_to_all.10.received, bf16[1536,256]{1,0:T(8,128)(2,1)S(1)} %copy-done), custom_call_target="tpu_custom_call" | custom-call | flops 1342177280 | bytes 2097152 | tf_op jit(solution)/shard_map/pallas_call | solution.py:360
  22.7 18.2 %all_to_all.11 = bf16[32,2,32,128]{3,2,1,0:T(8,128)(2,1)S(1)} all-to-all(bf16[32,2,32,128]{3,2,1,0:T(8,128)(2,1)S(1)} %shard_map.47), channel_id=1, replica_groups=mesh['shot'=16,'tm'=2] {'tm','shot'}, dimensions={0} | all-to-all | bytes 1048576 | tf_op jit(solution)/shard_map/all_to_all | solution.py:382
  40.9 0.8 %copy.8 = bf16[64,4,1024]{2,1,0:T(4,128)(2,1)} copy(bf16[64,4,1024]{2,1,0:T(4,128)(2,1)S(1)} %bitcast.11) | data formatting | bytes 1048576
Async XLA Ops:
  0.0 18.6 %copy-start = (bf16[1536,256]{1,0:T(8,128)(2,1)S(1)}, bf16[1536,256]{1,0:T(8,128)(2,1)}, u32[]{:S(2)}) copy-start(bf16[1536,256]{1,0:T(8,128)(2,1)} %constant.2.clone.tables) | copy-start | bytes 2359300

commit v11 on v10

--- a/solution.py
+++ b/solution.py
@@ -21,6 +21,7 @@
 HALF = WIN // 2
 SUB = 8
 TILE = 256
+NEAR = 4
 
 
 def bfloat_scale(table):
@@ -66,7 +67,8 @@
     shots, sources = TILE // (2 * windows * own), TILE // windows
     return (
         rearranging(
-            (blocks_of_time, shots, windows // blocks_of_time, 2, own), (1, 4, 3, 0, 2)
+            (blocks_of_time, NEAR, shots // NEAR, windows // blocks_of_time, 2, own),
+            (2, 1, 5, 4, 0, 3),
         ),
         rearranging((sources, windows), (1, 0)),
         rearranging((windows, sources), (1, 0)),
@@ -114,7 +116,7 @@
     lane_of_group = lax.broadcasted_iota(jnp.int32, (sources, HALF), 1)
     lane_of_some = lax.broadcasted_iota(jnp.int32, (some, HALF), 1)
 
-    senders = TILE // (rows * blocks_of_time)
+    planes, some_planes = shots // NEAR, TILE // (rows * blocks_of_time * NEAR)
     bounds = []
     for sweep in range(ITERS):
         limit = limits[sweep : sweep + 1, :] * kept_scale
@@ -128,8 +130,8 @@
     arrived = [
         jnp.concatenate(
             [
-                received[pl.ds(block * shots + chunk * senders, senders), r].reshape(-1, BLK)
-                for block in range(blocks_of_time)
+                received[pl.ds(side * planes + chunk * some_planes, some_planes), r].reshape(-1, BLK)
+                for side in range(blocks_of_time * NEAR)
             ],
             axis=0,
         )
@@ -285,7 +287,8 @@
             both = jnp.concatenate([pieces[0][side], pieces[1][side]], axis=1)
             both = both.astype(jnp.bfloat16)
             for k in range(sources // SUB):
-                target = block * shots + 2 * k + side
+                plane, near = divmod(2 * k + side, NEAR)
+                target = (block * NEAR + near) * planes + plane
                 out[target, r, inside * SUB : (inside + 2) * SUB, :] = both[k]
 
     for sweep in range(ITERS):
@@ -353,7 +356,19 @@
         ],
         compiler_params=pltpu.CompilerParams(vmem_limit_bytes=8 * 1024 * 1024),
     )(kept_far(sent), kept_far(delays.T), kept_far(thresholds))
-    received = lax.all_to_all(sent, ("tm", "shot"), split_axis=0, concat_axis=0, tiled=True)
+    order = [
+        (plane * NEAR + near) * blocks_of_time + block
+        for block in range(blocks_of_time)
+        for near in range(NEAR)
+        for plane in range(shots // NEAR)
+    ]
+
+    def exchanged(array):
+        return lax.all_to_all(
+            array, ("shot", "tm"), 0, 0, axis_index_groups=[order], tiled=True
+        )
+
+    received = exchanged(sent)
     tables, kept_scale = half_spectrum_tables()
     tables = np.concatenate(tables[:2] + order_tables(windows, own, blocks_of_time) + tables[2:], axis=0)
     held = SRC // shots
@@ -379,7 +394,7 @@
             transcendentals=ITERS * groups * SRC * HALF,
         ),
     )(delays, thresholds, received, jnp.asarray(tables))
-    final = lax.all_to_all(restored, ("tm", "shot"), split_axis=0, concat_axis=0, tiled=True)
+    final = exchanged(restored)
     final = final.reshape(receivers, blocks, held, BLK).transpose(0, 2, 1, 3)
     return final.reshape(receivers, held, samples)
 
@@ -521,6 +536,7 @@
     held, windows = SRC // shots, samples // WIN
     return (
         receivers % (shots * blocks_of_time) == 0
+        and shots % (2 * NEAR) == 0
         and held * 2 == SUB
         and windows % 2 == 0
         and windows * blocks_of_time == SUB

time: 41.9 us -> 41.2 us (0.983)
  the two profiles are of different devices: /device:TPU:0 before, /device:TPU:1 now
where the time goes in v11:
time: 41.2 us; the launch traced here: 41 us
  blocking collectives  34.9 us (85%)
  Pallas kernels  5.27 us (13%)
  local copies, waits for them, and re-layouts  0.8 us (2%)
    all_to_all x2, blocking collectives, exchanged(): lax.all_to_all(array, ('shot', 'tm'), 0, 0, axis_index_groups=[order], ti...  34.9 us
    pallas_call x1, Pallas kernels, gathers_of_all_samples(): pl.pallas_call(functools.partial(gather_kernel, shots, float(kept_scale))...  4.1 us
    pallas_call x1, Pallas kernels, gathers_of_all_samples(): pl.pallas_call(cast_kernel, out_shape=(jax.ShapeDtypeStruct(sent.shape, j...  1.17 us

profile of v11, /device:TPU:1, one launch (start us, length us, event | category | flops | bytes accessed | tf_op | source)
XLA Modules:
  0.0 41.0 jit_solution(1374802627982625940)
XLA Ops:
  0.0 0.0 copy-start
  0.0 1.2 %shard_map.46 = (bf16[32,2,16,128]{3,2,1,0:T(8,128)(2,1)S(1)}, s32[2,32]{1,0:T(2,128)S(1)}, f32[2,64]{1,0:T(2,128)S(1)}) custom-call(f32[32,2,16,128]{3,2,1,0:T(8,128)} %bitcast.12, s32[2,32]{1,0:T(2,128)} %bitcast.13, f32[2,64]{1,0:T(2,128)} %limits.1), custom_call_target="tpu_custom_call" | custom-call | tf_op jit(solution)/shard_map/pallas_call | solution.py:344
  1.2 17.2 %all_to_all.10.received = bf16[32,2,16,128]{3,2,1,0:T(8,128)(2,1)S(1)} all-to-all(bf16[32,2,16,128]{3,2,1,0:T(8,128)(2,1)S(1)} %get-tuple-element.10), channel_id=1, replica_groups={{0,8,16,24,2,10,18,26,4,12,20,28,6,14,22,30,1,9,17,25,3,11,19,27,5,13,2..., dimensions={0} | all-to-all | bytes 524288 | tf_op jit(solution)/shard_map/all_to_all | solution.py:367
  18.4 0.0 copy-done
  18.4 4.1 %shard_map.47 = bf16[32,2,32,128]{3,2,1,0:T(8,128)(2,1)S(1)} custom-call(s32[2,32]{1,0:T(2,128)S(1)} %get-tuple-element.8.delays_far, f32[2,64]{1,0:T(2,128)S(1)} %get-tuple-element.9.limits, bf16[32,2,16,128]{3,2,1,0:T(8,128)(2,1)S(1)} %all_to_all.10.received, bf16[1536,256]{1,0:T(8,128)(2,1)S(1)} %copy-done), custom_call_target="tpu_custom_call" | custom-call | flops 1342177280 | bytes 2097152 | tf_op jit(solution)/shard_map/pallas_call | solution.py:375
  22.5 17.7 %all_to_all.11 = bf16[32,2,32,128]{3,2,1,0:T(8,128)(2,1)S(1)} all-to-all(bf16[32,2,32,128]{3,2,1,0:T(8,128)(2,1)S(1)} %shard_map.47), channel_id=1, replica_groups={{0,8,16,24,2,10,18,26,4,12,20,28,6,14,22,30,1,9,17,25,3,11,19,27,5,13,2..., dimensions={0} | all-to-all | bytes 1048576 | tf_op jit(solution)/shard_map/all_to_all | solution.py:367
  40.2 0.8 %copy.8 = bf16[64,4,1024]{2,1,0:T(4,128)(2,1)} copy(bf16[64,4,1024]{2,1,0:T(4,128)(2,1)S(1)} %bitcast.11) | data formatting | bytes 1048576
Async XLA Ops:
  0.0 18.4 %copy-start = (bf16[1536,256]{1,0:T(8,128)(2,1)S(1)}, bf16[1536,256]{1,0:T(8,128)(2,1)}, u32[]{:S(2)}) copy-start(bf16[1536,256]{1,0:T(8,128)(2,1)} %constant.2.clone.tables) | copy-start | bytes 2359300

commit v12 on v11

--- a/solution.py
+++ b/solution.py
@@ -67,8 +67,8 @@
     shots, sources = TILE // (2 * windows * own), TILE // windows
     return (
         rearranging(
-            (blocks_of_time, NEAR, shots // NEAR, windows // blocks_of_time, 2, own),
-            (2, 1, 5, 4, 0, 3),
+            (NEAR, blocks_of_time, shots // NEAR, windows // blocks_of_time, 2, own),
+            (2, 0, 5, 4, 1, 3),
         ),
         rearranging((sources, windows), (1, 0)),
         rearranging((windows, sources), (1, 0)),
@@ -288,7 +288,7 @@
             both = both.astype(jnp.bfloat16)
             for k in range(sources // SUB):
                 plane, near = divmod(2 * k + side, NEAR)
-                target = (block * NEAR + near) * planes + plane
+                target = (near * blocks_of_time + block) * planes + plane
                 out[target, r, inside * SUB : (inside + 2) * SUB, :] = both[k]
 
     for sweep in range(ITERS):
@@ -358,8 +358,8 @@
     )(kept_far(sent), kept_far(delays.T), kept_far(thresholds))
     order = [
         (plane * NEAR + near) * blocks_of_time + block
+        for near in range(NEAR)
         for block in range(blocks_of_time)
-        for near in range(NEAR)
         for plane in range(shots // NEAR)
     ]
 

time: 41.2 us -> 41.6 us (level)
  no operation moved by 1% of the time
where the time goes in v12:
time: 41.6 us; the launch traced here: 41.3 us
  blocking collectives  35.2 us (85%)
  Pallas kernels  5.27 us (13%)
  local copies, waits for them, and re-layouts  0.8 us (2%)
    all_to_all x2, blocking collectives, exchanged(): lax.all_to_all(array, ('shot', 'tm'), 0, 0, axis_index_groups=[order], ti...  35.2 us
    pallas_call x1, Pallas kernels, gathers_of_all_samples(): pl.pallas_call(functools.partial(gather_kernel, shots, float(kept_scale))...  4.1 us
    pallas_call x1, Pallas kernels, gathers_of_all_samples(): pl.pallas_call(cast_kernel, out_shape=(jax.ShapeDtypeStruct(sent.shape, j...  1.17 us

profile of v12, /device:TPU:1, one launch (start us, length us, event | category | flops | bytes accessed | tf_op | source)
XLA Modules:
  0.0 41.3 jit_solution(2662866625767755147)
XLA Ops:
  0.0 0.0 copy-start
  0.0 1.2 %shard_map.46 = (bf16[32,2,16,128]{3,2,1,0:T(8,128)(2,1)S(1)}, s32[2,32]{1,0:T(2,128)S(1)}, f32[2,64]{1,0:T(2,128)S(1)}) custom-call(f32[32,2,16,128]{3,2,1,0:T(8,128)} %bitcast.12, s32[2,32]{1,0:T(2,128)} %bitcast.13, f32[2,64]{1,0:T(2,128)} %limits.1), custom_call_target="tpu_custom_call" | custom-call | tf_op jit(solution)/shard_map/pallas_call | solution.py:344
  1.2 17.5 %all_to_all.10.received = bf16[32,2,16,128]{3,2,1,0:T(8,128)(2,1)S(1)} all-to-all(bf16[32,2,16,128]{3,2,1,0:T(8,128)(2,1)S(1)} %get-tuple-element.10), channel_id=1, replica_groups={{0,8,16,24,1,9,17,25,2,10,18,26,3,11,19,27,4,12,20,28,5,13,21,29,6,14,2..., dimensions={0} | all-to-all | bytes 524288 | tf_op jit(solution)/shard_map/all_to_all | solution.py:367
  18.7 0.0 copy-done
  18.7 4.1 %shard_map.47 = bf16[32,2,32,128]{3,2,1,0:T(8,128)(2,1)S(1)} custom-call(s32[2,32]{1,0:T(2,128)S(1)} %get-tuple-element.8.delays_far, f32[2,64]{1,0:T(2,128)S(1)} %get-tuple-element.9.limits, bf16[32,2,16,128]{3,2,1,0:T(8,128)(2,1)S(1)} %all_to_all.10.received, bf16[1536,256]{1,0:T(8,128)(2,1)S(1)} %copy-done), custom_call_target="tpu_custom_call" | custom-call | flops 1342177280 | bytes 2097152 | tf_op jit(solution)/shard_map/pallas_call | solution.py:375
  22.8 17.7 %all_to_all.11 = bf16[32,2,32,128]{3,2,1,0:T(8,128)(2,1)S(1)} all-to-all(bf16[32,2,32,128]{3,2,1,0:T(8,128)(2,1)S(1)} %shard_map.47), channel_id=1, replica_groups={{0,8,16,24,1,9,17,25,2,10,18,26,3,11,19,27,4,12,20,28,5,13,21,29,6,14,2..., dimensions={0} | all-to-all | bytes 1048576 | tf_op jit(solution)/shard_map/all_to_all | solution.py:367
  40.5 0.8 %copy.8 = bf16[64,4,1024]{2,1,0:T(4,128)(2,1)} copy(bf16[64,4,1024]{2,1,0:T(4,128)(2,1)S(1)} %bitcast.11) | data formatting | bytes 1048576
Async XLA Ops:
  0.0 18.7 %copy-start = (bf16[1536,256]{1,0:T(8,128)(2,1)S(1)}, bf16[1536,256]{1,0:T(8,128)(2,1)}, u32[]{:S(2)}) copy-start(bf16[1536,256]{1,0:T(8,128)(2,1)} %constant.2.clone.tables) | copy-start | bytes 2359300
